TPU v7x, 512 devices: a whole 4x4x16 slice. The times are simulated.
512 devices in a mesh: gx: 4 (over z_lo), gy: 4 (over z_hi), gz: 32 (over x, y, core).
Axes of the slice: x: 4, y: 4, z: 16 (z_hi: 4, z_lo: 4; z = z_hi * 4 + z_lo), core: 2. Of those that a mesh axis runs over, the one named last changes fastest.
Arguments:
- heat_level: float32 [32, 64, 4096], P('gx', 'gy', 'gz'), may hold values from 0 to 1
- flow_rate: float32 [3, 32, 64, 4096], P(None, 'gx', 'gy', 'gz'), may hold values from -9 to 9
- flow_guess: float32 [4, 32, 64, 4096], P(None, 'gx', 'gy', 'gz'), may hold values from -6 to 6
- rock_label: int32 [32, 64, 4096], P('gx', 'gy', 'gz'), may hold values from 0 to 3
- clamp_mask: int32 [32, 64, 4096], P('gx', 'gy', 'gz'), may hold values from 0 to 15
- rheology_coefficient: float32 [4], replicated, may hold values from 0.3 to 3
- local_operator_tiles: float32 [3, 32, 32], replicated, may hold values from -1 to 1
Outputs:
- heat_level_later: float32 [32, 64, 4096], P('gx', 'gy', 'gz')
- equation_misfit: float32 [4, 32, 64, 4096], P(None, 'gx', 'gy', 'gz')
All inputs are finite; a program needn't handle non-finite values. Where the computation divides by a largest or mean magnitude, that divisor is 1e-20 or more.
Results may differ from a plain program's by a relative error of at most 0.0003.
Values sent between devices are 32-bit elements; how exact they have to be, the bound alone decides.
A program may use at most 64 MiB of HBM per device.

v0:
```python
import jax
import jax.numpy as jnp
from jax import lax
from jax.sharding import PartitionSpec as P

COURANT = 0.5
DIFFUSIVITY = 1.0
ACTIVATION = 3.0
STABILIZER = 0.25
THERMAL_LIFT = 2.0
CORNERS = tuple(((a, b, c) for a in (0, 1) for b in (0, 1) for c in (0, 1)))


def with_halo(cells, sides, width):
    for axis, dim in sides:
        count = lax.axis_size(axis)
        ends = count - 1
        head = lax.slice_in_dim(cells, 0, width, axis=dim)
        tail = lax.slice_in_dim(cells, cells.shape[dim] - width, cells.shape[dim], axis=dim)
        cells = jnp.concatenate(
            [
                lax.ppermute(tail, axis, [(i, (i + 1) % count) for i in range(ends)]),
                cells,
                lax.ppermute(head, axis, [((i + 1) % count, i) for i in range(ends)]),
            ],
            axis=dim,
        )
    return cells


def lookup(rock_label, rheology_coefficient):
    total = jnp.zeros(rock_label.shape, jnp.float32)
    for selector in range(rheology_coefficient.shape[0]):
        total = total + jnp.where(rock_label == selector, rheology_coefficient[selector], 0.0)
    return total


def advance_heat(bordered_copy, flow_rate, duration_delta):
    centre = bordered_copy[1:-1, 1:-1, 1:-1]
    plus_x = bordered_copy[2:, 1:-1, 1:-1]
    minus_x = bordered_copy[:-2, 1:-1, 1:-1]
    plus_y = bordered_copy[1:-1, 2:, 1:-1]
    minus_y = bordered_copy[1:-1, :-2, 1:-1]
    plus_z = bordered_copy[1:-1, 1:-1, 2:]
    minus_z = bordered_copy[1:-1, 1:-1, :-2]
    laplace = plus_x + minus_x + plus_y + minus_y + plus_z + minus_z - 6.0 * centre
    transport = (
        flow_rate[0] * (plus_x - minus_x)
        + flow_rate[1] * (plus_y - minus_y)
        + flow_rate[2] * (plus_z - minus_z)
    )
    return centre + duration_delta * (DIFFUSIVITY * laplace - 0.5 * transport)


def element_stiffness(widened, local_operator_tiles, valid_cells):
    span_x, span_y, span_z = valid_cells.shape

    def corner(field, offset):
        return field[
            offset[0] : offset[0] + span_x,
            offset[1] : offset[1] + span_y,
            offset[2] : offset[2] + span_z,
        ]

    tcell = sum((corner(widened[0], offset) for offset in CORNERS)) / 8.0
    prefac = jnp.where(valid_cells, widened[1][:span_x, :span_y, :span_z], 1.0)
    viscosity = prefac * jnp.exp(ACTIVATION * (0.5 - tcell))
    stabilize = STABILIZER / viscosity
    element_values = jnp.stack(
        [corner(widened[2 + k], offset) for k in range(4) for offset in CORNERS]
    )
    forces = viscosity * jnp.einsum(
        "ab,bxyz->axyz", local_operator_tiles[0], element_values, precision=lax.Precision.HIGHEST
    )
    forces = forces + stabilize * jnp.einsum(
        "ab,bxyz->axyz", local_operator_tiles[1], element_values, precision=lax.Precision.HIGHEST
    )
    forces = forces + jnp.einsum(
        "ab,bxyz->axyz", local_operator_tiles[2], element_values, precision=lax.Precision.HIGHEST
    )
    forces = jnp.where(valid_cells[None], forces, 0.0)
    owned_x, owned_y, owned_z = (span_x - 1, span_y - 1, span_z - 1)
    rows = []
    for k in range(4):
        summed = jnp.zeros((owned_x, owned_y, owned_z), jnp.float32)
        for q, (a, b, c) in enumerate(CORNERS):
            summed = (
                summed
                + forces[
                    k * 8 + q,
                    1 - a : 1 - a + owned_x,
                    1 - b : 1 - b + owned_y,
                    1 - c : 1 - c + owned_z,
                ]
            )
        rows.append(summed)
    return jnp.stack(rows)


def shards(
    heat_level,
    flow_rate,
    flow_guess,
    rock_label,
    clamp_mask,
    rheology_coefficient,
    local_operator_tiles,
):
    lateral_span_x, lateral_span_y, vertical_span = heat_level.shape
    top_speed = lax.pmax(jnp.max(jnp.abs(flow_rate)), ("gx", "gy", "gz"))
    duration_delta = COURANT / (top_speed + 6.0 * DIFFUSIVITY)
    local_coefficient = lookup(rock_label, rheology_coefficient)
    bordered_copy = with_halo(heat_level, (("gx", 0), ("gy", 1), ("gz", 2)), 1)
    heat_level_later = advance_heat(bordered_copy, flow_rate, duration_delta)
    layered_arrays = jnp.concatenate(
        [heat_level_later[None], local_coefficient[None], flow_guess], 0
    )
    widened = with_halo(layered_arrays, (("gx", 1), ("gy", 2), ("gz", 3)), 1)
    first_x = (
        lax.axis_index("gx") * lateral_span_x + jnp.arange(lateral_span_x + 1, dtype=jnp.int32) - 1
    )
    first_y = (
        lax.axis_index("gy") * lateral_span_y + jnp.arange(lateral_span_y + 1, dtype=jnp.int32) - 1
    )
    first_z = (
        lax.axis_index("gz") * vertical_span + jnp.arange(vertical_span + 1, dtype=jnp.int32) - 1
    )
    valid_x = (first_x >= 0) & (first_x <= lateral_span_x * lax.axis_size("gx") - 2)
    valid_y = (first_y >= 0) & (first_y <= lateral_span_y * lax.axis_size("gy") - 2)
    valid_z = (first_z >= 0) & (first_z <= vertical_span * lax.axis_size("gz") - 2)
    valid_cells = valid_x[:, None, None] & valid_y[None, :, None] & valid_z[None, None, :]
    stiffness = element_stiffness(widened, local_operator_tiles, valid_cells)
    unknown_position = jnp.arange(4, dtype=jnp.int32).reshape(4, 1, 1, 1)
    source_term = THERMAL_LIFT * heat_level_later[None] * (unknown_position == 2)
    fixed_dof = clamp_mask[None] // 2**unknown_position % 2 == 1
    equation_misfit = jnp.where(fixed_dof, flow_guess, stiffness - source_term)
    return (heat_level_later, equation_misfit)


def solution(mesh):
    in_specs = (
        P("gx", "gy", "gz"),
        P(None, "gx", "gy", "gz"),
        P(None, "gx", "gy", "gz"),
        P("gx", "gy", "gz"),
        P("gx", "gy", "gz"),
        P(),
        P(),
    )
    out_specs = (P("gx", "gy", "gz"), P(None, "gx", "gy", "gz"))
    return jax.shard_map(shards, mesh=mesh, in_specs=in_specs, out_specs=out_specs, check_vma=False)
```

profile of v0, /device:TPU:1, one launch (start us, length us, event | category | flops | bytes accessed | tf_op | source)
XLA Modules:
  0.0 241.1 jit_solution(16624561162549272364)
XLA Ops:
  0.6 0.7 fusion.32
  1.4 4.4 %collective-permute-start.1 = (f32[1,16,128]{2,1,0:T(8,128)S(1)}, f32[1,16,128]{2,1,0:T(8,128)S(1)}, u32[]{:S(2)}, u32[]{:S(2)}) collective-permute-start(f32[1,16,128]{2,1,0:T(8,128)S(1)} %get-tuple-element.63), channel_id=1, source_target_pairs={{0,128},{128,256},{256,384},{1,129},{129,257},{257,385},{2,130},{1... | collective-permute-start | bytes 24584 | tf_op jit(solution)/shard_map/ppermute | solution.py:22
  5.8 1.3 collective-permute-start
  7.1 1.5 fusion.33
  8.6 3.5 %add_bitcast_fusion = f32[1,8,16,128]{3,2,1,0:T(8,128)S(1)} fusion(s32[8,16,128]{2,1,0:T(8,128)} %param.10, f32[]{:T(128)} %bitcast.7, f32[]{:T(128)} %bitcast.6, f32[]{:T(128)} %bitcast.5, f32[]{:T(128)} %bitcast.4), kind=kLoop, calls=%fused_computation.114 | loop fusion | flops 180224 | bytes 131088 | tf_op jit(solution)/shard_map/broadcast_in_dim | solution.py:116
  12.1 0.8 constant_dynamic-update-slice_fusion.1
  13.0 1.3 collective-permute-start.2
  14.3 9.4 %collective-permute-start.3 = (f32[10,1,128]{2,1,0:T(1,128)S(1)}, f32[10,1,128]{2,1,0:T(1,128)S(1)}, u32[]{:S(2)}, u32[]{:S(2)}) collective-permute-start(f32[10,1,128]{2,1,0:T(1,128)S(1)} %get-tuple-element.60), channel_id=1, source_target_pairs={{0,32},{32,64},{64,96},{1,33},{33,65},{65,97},{2,34},{34,66},{66,9... | collective-permute-start | bytes 15368 | tf_op jit(solution)/shard_map/ppermute | solution.py:22
  23.7 1.5 abs_reduce_fusion
  25.4 4.7 %collective-permute-start.4 = (f32[10,18,1]{2,1,0:T(8,128)S(1)}, f32[10,18,1]{2,1,0:T(8,128)S(1)}, u32[]{:S(2)}, u32[]{:S(2)}) collective-permute-start(f32[10,18,1]{2,1,0:T(8,128)S(1)} %get-tuple-element.58), channel_id=1, source_target_pairs={{1,0},{2,1},{3,2},{4,3},{5,4},{6,5},{7,6},{8,7},{9,8},{10,9},{11,1... | collective-permute-start | bytes 2168 | tf_op jit(solution)/shard_map/ppermute | solution.py:24
  30.1 1.9 collective-permute-start.5
  32.1 111.6 %pmax.7 = f32[]{:T(128)} all-reduce(f32[]{:T(128)} %abs_reduce_fusion), channel_id=1, replica_groups=mesh['gx'=4,'gy'=4,'gz'=32] {'gx','gy','gz'}, use_global_device_ids=true, to_apply=%region_1.0 | all-reduce | flops 1 | bytes 8 | tf_op jit(solution)/shard_map/pmax | solution.py:110
  144.4 1.2 broadcast_multiply_fusion
  145.6 0.8 pad_maximum_fusion.15
  146.4 2.6 %collective-permute-start.6 = (f32[6,1,16,128]{3,2,1,0:T(8,128)S(1)}, f32[6,1,16,128]{3,2,1,0:T(8,128)S(1)}, u32[]{:S(2)}, u32[]{:S(2)}) collective-permute-start(f32[6,1,16,128]{3,2,1,0:T(8,128)S(1)} %get-tuple-element.24), channel_id=1, source_target_pairs={{0,128},{128,256},{256,384},{1,129},{129,257},{257,385},{2,130},{1... | collective-permute-start | bytes 147464 | tf_op jit(solution)/shard_map/ppermute | solution.py:22
  149.0 1.3 collective-permute-start.7
  151.0 2.8 %collective-permute-done.7 = f32[6,1,16,128]{3,2,1,0:T(8,128)S(1)} collective-permute-done((f32[6,1,16,128]{3,2,1,0:T(8,128)S(1)}, f32[6,1,16,128]{3,2,1,0:T(8,128)S(1)}, u32[]{:S(2)}, u32[]{:S(2)}) %collective-permute-start.7) | collective-permute-done | bytes 49184 | tf_op jit(solution)/shard_map/ppermute | solution.py:24
  153.8 1.0 pad_maximum_fusion.20
  154.8 2.8 %collective-permute-start.8 = (f32[6,10,1,128]{3,2,1,0:T(1,128)S(1)}, f32[6,10,1,128]{3,2,1,0:T(1,128)S(1)}, u32[]{:S(2)}, u32[]{:S(2)}) collective-permute-start(f32[6,10,1,128]{3,2,1,0:T(1,128)S(1)} %get-tuple-element.22), channel_id=1, source_target_pairs={{0,32},{32,64},{64,96},{1,33},{33,65},{65,97},{2,34},{34,66},{66,9... | collective-permute-start | bytes 92168 | tf_op jit(solution)/shard_map/ppermute | solution.py:22
  157.6 1.3 collective-permute-start.9
  159.5 7.3 %collective-permute-done.9 = f32[6,10,1,128]{3,2,1,0:T(1,128)S(1)} collective-permute-done((f32[6,10,1,128]{3,2,1,0:T(1,128)S(1)}, f32[6,10,1,128]{3,2,1,0:T(1,128)S(1)}, u32[]{:S(2)}, u32[]{:S(2)}) %collective-permute-start.9) | collective-permute-done | bytes 30752 | tf_op jit(solution)/shard_map/ppermute | solution.py:24
  166.8 1.1 pad_maximum_fusion.1
  168.6 5.8 %collective-permute-start.10 = (f32[6,10,18,1]{2,3,1,0:T(1,128)S(1)}, f32[6,10,18,1]{2,3,1,0:T(1,128)S(1)}, u32[]{:S(2)}, u32[]{:S(2)}) collective-permute-start(f32[6,10,18,1]{2,3,1,0:T(1,128)S(1)} %copy.42), channel_id=1, source_target_pairs={{0,1},{1,2},{2,3},{3,4},{4,5},{5,6},{6,7},{7,8},{8,9},{9,10},{10,1... | collective-permute-start | bytes 12968 | tf_op jit(solution)/shard_map/ppermute | solution.py:22
  174.9 1.9 collective-permute-start.11
  178.5 1.6 collective-permute-done.11
  180.6 0.9 pad_maximum_fusion
  185.7 0.8 copy.63
  186.5 0.8 copy.64
  187.3 0.8 copy.65
  188.1 0.8 copy.66
  189.0 0.8 copy.67
  189.8 0.8 copy.68
  190.6 0.8 copy.69
  191.8 0.8 copy.46
  192.6 0.8 copy.47
  193.4 0.8 copy.48
  194.3 0.8 copy.49
  195.1 0.8 copy.50
  195.9 0.8 copy.51
  196.7 0.8 copy.52
  197.6 0.8 copy.53
  198.4 17.6 %stack.138 = f32[32,9,17,129]{3,0,2,1:T(8,128)} concatenate(f32[1,9,17,129]{3,0,2,1:T(1,128)} %copy.46, f32[1,9,17,129]{3,0,2,1:T(1,128)} %copy.47, f32[1,9,17,129]{3,0,2,1:T(1,128)} %copy.48, f32[1,9,17,129]{3,0,2,1:T(1,128)} %copy.49, f32[1,9,17,129]{3,0,2,1:T(1,128)} %copy.50, f32[1,9,17,129]{3,0,2,1:T(1,128)} %copy.51, f32[1,9,17,129]{3,0,2,1:T(1,128)} %copy.52, ...), dimensions={0} | concatenate | bytes 5052672 | tf_op jit(solution)/shard_map/stack | solution.py:69
  216.0 6.4 %fusion.16 = f32[9,17,129,32]{2,3,1,0:T(8,128)S(1)} fusion(f32[32,9,17,129]{3,0,2,1:T(8,128)} %stack.138, f32[3,32,32]{2,1,0:T(8,128)} %param.13), kind=kOutput, calls=%fused_computation.125 | convolution fusion | flops 242528256 | bytes 7556224 | tf_op jit(solution)/shard_map/ab,bxyz->axyz/dot_general | solution.py:75
  222.4 4.4 %fusion.18 = f32[9,17,129,32]{2,3,1,0:T(8,128)S(1)} fusion(f32[32,9,17,129]{3,0,2,1:T(8,128)S(1)} %copy-done, f32[3,32,32]{2,1,0:T(8,128)S(1)} %copy-done.6), kind=kOutput, calls=%fused_computation.127 | convolution fusion | flops 242528256 | bytes 7556224 | tf_op jit(solution)/shard_map/ab,bxyz->axyz/dot_general | solution.py:72
  226.9 5.3 %select_bitcast_fusion = f32[32,9,17,129]{3,0,2,1:T(8,128)S(1)} fusion(f32[9,17,129,32]{2,3,1,0:T(8,128)S(1)} %fusion.16, f32[9,17,129,32]{2,3,1,0:T(8,128)S(1)} %fusion.18, f32[9,17,129]{2,1,0:T(8,128)S(1)} %get-tuple-element.8, f32[9,17,129]{2,1,0:T(8,128)S(1)} %get-tuple-element.9, pred[9,17,129]{2,1,0:T(8,128)(4,1)S(1)} %copy-done.5, ...), kind=kOutput, calls=%fused_computation | convolution fusion | flops 245686176 | bytes 18080896 | tf_op jit(solution)/shard_map/ab,bxyz->axyz/dot_general | solution.py:78
  232.2 1.1 slice_add_fusion.28
  233.3 1.4 slice_add_fusion.21
  234.7 5.7 %fusion.2 = f32[4,8,16,128]{3,0,2,1:T(4,128)S(1)} fusion(f32[1,8,16,128]{3,0,2,1:T(1,128)S(1)} %get-tuple-element.11, f32[1,8,16,128]{3,0,2,1:T(1,128)S(1)} %get-tuple-element.13, f32[1,8,16,128]{3,0,2,1:T(1,128)S(1)} %get-tuple-element.12, f32[1,8,16,128]{3,0,2,1:T(1,128)S(1)} %get-tuple-element.10, f32[4,8,16,128]{3,2,1,0:T(8,128)S(1)} %copy-done.1, ...), kind=kLoop, calls=%fused_computation.10 | loop fusion | flops 1638400 | bytes 983088 | tf_op jit(solution)/shard_map/jit(_where)/select_n | solution.py:136
  (67 shorter events, 9.9 us)
Async XLA Ops:
  0.6 176.7 %copy-start.3 = (s32[8,16,128]{2,1,0:T(8,128)S(1)}, s32[8,16,128]{2,1,0:T(8,128)}, u32[]{:S(2)}) copy-start(s32[8,16,128]{2,1,0:T(8,128)} %param.11) | copy-start | bytes 196612
  1.4 10.7 %collective-permute-start.1 = (f32[1,16,128]{2,1,0:T(8,128)S(1)}, f32[1,16,128]{2,1,0:T(8,128)S(1)}, u32[]{:S(2)}, u32[]{:S(2)}) collective-permute-start(f32[1,16,128]{2,1,0:T(8,128)S(1)} %get-tuple-element.63), channel_id=1, source_target_pairs={{0,128},{128,256},{256,384},{1,129},{129,257},{257,385},{2,130},{1... | collective-permute-start | bytes 24584 | tf_op jit(solution)/shard_map/ppermute | solution.py:22
  5.8 7.2 %collective-permute-start = (f32[1,16,128]{2,1,0:T(8,128)S(1)}, f32[1,16,128]{2,1,0:T(8,128)S(1)}, u32[]{:S(2)}, u32[]{:S(2)}) collective-permute-start(f32[1,16,128]{2,1,0:T(8,128)S(1)} %get-tuple-element.62), channel_id=1, source_target_pairs={{128,0},{256,128},{384,256},{129,1},{257,129},{385,257},{130,2},{2... | collective-permute-start | bytes 24584 | tf_op jit(solution)/shard_map/ppermute | solution.py:24
  13.0 12.3 %collective-permute-start.2 = (f32[10,1,128]{2,1,0:T(1,128)S(1)}, f32[10,1,128]{2,1,0:T(1,128)S(1)}, u32[]{:S(2)}, u32[]{:S(2)}) collective-permute-start(f32[10,1,128]{2,1,0:T(1,128)S(1)} %get-tuple-element.61), channel_id=1, source_target_pairs={{32,0},{64,32},{96,64},{33,1},{65,33},{97,65},{34,2},{66,34},{98,6... | collective-permute-start | bytes 15368 | tf_op jit(solution)/shard_map/ppermute | solution.py:24
  14.3 11.0 %collective-permute-start.3 = (f32[10,1,128]{2,1,0:T(1,128)S(1)}, f32[10,1,128]{2,1,0:T(1,128)S(1)}, u32[]{:S(2)}, u32[]{:S(2)}) collective-permute-start(f32[10,1,128]{2,1,0:T(1,128)S(1)} %get-tuple-element.60), channel_id=1, source_target_pairs={{0,32},{32,64},{64,96},{1,33},{33,65},{65,97},{2,34},{34,66},{66,9... | collective-permute-start | bytes 15368 | tf_op jit(solution)/shard_map/ppermute | solution.py:22
  25.3 155.3 %copy-start.1 = (f32[4,8,16,128]{3,2,1,0:T(8,128)S(1)}, f32[4,8,16,128]{3,2,1,0:T(8,128)}, u32[]{:S(2)}) copy-start(f32[4,8,16,128]{3,2,1,0:T(8,128)} %param.9) | copy-start | bytes 786436
  25.4 119.0 %collective-permute-start.4 = (f32[10,18,1]{2,1,0:T(8,128)S(1)}, f32[10,18,1]{2,1,0:T(8,128)S(1)}, u32[]{:S(2)}, u32[]{:S(2)}) collective-permute-start(f32[10,18,1]{2,1,0:T(8,128)S(1)} %get-tuple-element.58), channel_id=1, source_target_pairs={{1,0},{2,1},{3,2},{4,3},{5,4},{6,5},{7,6},{8,7},{9,8},{10,9},{11,1... | collective-permute-start | bytes 2168 | tf_op jit(solution)/shard_map/ppermute | solution.py:24
  30.1 114.3 %collective-permute-start.5 = (f32[10,18,1]{2,1,0:T(8,128)S(1)}, f32[10,18,1]{2,1,0:T(8,128)S(1)}, u32[]{:S(2)}, u32[]{:S(2)}) collective-permute-start(f32[10,18,1]{2,1,0:T(8,128)S(1)} %get-tuple-element.59), channel_id=1, source_target_pairs={{0,1},{1,2},{2,3},{3,4},{4,5},{5,6},{6,7},{7,8},{8,9},{9,10},{10,1... | collective-permute-start | bytes 2168 | tf_op jit(solution)/shard_map/ppermute | solution.py:22
  145.6 36.0 %copy-start.2 = (f32[8,16,128]{2,1,0:T(8,128)}, f32[8,16,128]{2,1,0:T(8,128)S(1)}, u32[]{:S(2)}) copy-start(f32[8,16,128]{2,1,0:T(8,128)S(1)} %get-tuple-element.7) | copy-start | bytes 196612
  146.4 4.6 %collective-permute-start.6 = (f32[6,1,16,128]{3,2,1,0:T(8,128)S(1)}, f32[6,1,16,128]{3,2,1,0:T(8,128)S(1)}, u32[]{:S(2)}, u32[]{:S(2)}) collective-permute-start(f32[6,1,16,128]{3,2,1,0:T(8,128)S(1)} %get-tuple-element.24), channel_id=1, source_target_pairs={{0,128},{128,256},{256,384},{1,129},{129,257},{257,385},{2,130},{1... | collective-permute-start | bytes 147464 | tf_op jit(solution)/shard_map/ppermute | solution.py:22
  149.0 4.8 %collective-permute-start.7 = (f32[6,1,16,128]{3,2,1,0:T(8,128)S(1)}, f32[6,1,16,128]{3,2,1,0:T(8,128)S(1)}, u32[]{:S(2)}, u32[]{:S(2)}) collective-permute-start(f32[6,1,16,128]{3,2,1,0:T(8,128)S(1)} %get-tuple-element.25), channel_id=1, source_target_pairs={{128,0},{256,128},{384,256},{129,1},{257,129},{385,257},{130,2},{2... | collective-permute-start | bytes 147464 | tf_op jit(solution)/shard_map/ppermute | solution.py:24
  154.8 4.7 %collective-permute-start.8 = (f32[6,10,1,128]{3,2,1,0:T(1,128)S(1)}, f32[6,10,1,128]{3,2,1,0:T(1,128)S(1)}, u32[]{:S(2)}, u32[]{:S(2)}) collective-permute-start(f32[6,10,1,128]{3,2,1,0:T(1,128)S(1)} %get-tuple-element.22), channel_id=1, source_target_pairs={{0,32},{32,64},{64,96},{1,33},{33,65},{65,97},{2,34},{34,66},{66,9... | collective-permute-start | bytes 92168 | tf_op jit(solution)/shard_map/ppermute | solution.py:22
  157.6 9.2 %collective-permute-start.9 = (f32[6,10,1,128]{3,2,1,0:T(1,128)S(1)}, f32[6,10,1,128]{3,2,1,0:T(1,128)S(1)}, u32[]{:S(2)}, u32[]{:S(2)}) collective-permute-start(f32[6,10,1,128]{3,2,1,0:T(1,128)S(1)} %get-tuple-element.23), channel_id=1, source_target_pairs={{32,0},{64,32},{96,64},{33,1},{65,33},{97,65},{34,2},{66,34},{98,6... | collective-permute-start | bytes 92168 | tf_op jit(solution)/shard_map/ppermute | solution.py:24
  168.6 9.4 %collective-permute-start.10 = (f32[6,10,18,1]{2,3,1,0:T(1,128)S(1)}, f32[6,10,18,1]{2,3,1,0:T(1,128)S(1)}, u32[]{:S(2)}, u32[]{:S(2)}) collective-permute-start(f32[6,10,18,1]{2,3,1,0:T(1,128)S(1)} %copy.42), channel_id=1, source_target_pairs={{0,1},{1,2},{2,3},{3,4},{4,5},{5,6},{6,7},{7,8},{8,9},{9,10},{10,1... | collective-permute-start | bytes 12968 | tf_op jit(solution)/shard_map/ppermute | solution.py:22
  174.9 5.2 %collective-permute-start.11 = (f32[6,10,18,1]{2,3,1,0:T(1,128)S(1)}, f32[6,10,18,1]{2,3,1,0:T(1,128)S(1)}, u32[]{:S(2)}, u32[]{:S(2)}) collective-permute-start(f32[6,10,18,1]{2,3,1,0:T(1,128)S(1)} %copy.43), channel_id=1, source_target_pairs={{1,0},{2,1},{3,2},{4,3},{5,4},{6,5},{7,6},{8,7},{9,8},{10,9},{11,1... | collective-permute-start | bytes 12968 | tf_op jit(solution)/shard_map/ppermute | solution.py:24
  216.0 6.5 %copy-start = (f32[32,9,17,129]{3,0,2,1:T(8,128)S(1)}, f32[32,9,17,129]{3,0,2,1:T(8,128)}, u32[]{:S(2)}) copy-start(f32[32,9,17,129]{3,0,2,1:T(8,128)} %stack.138) | copy-start | bytes 7579012
  216.0 6.5 %copy-start.6 = (f32[3,32,32]{2,1,0:T(8,128)S(1)}, f32[3,32,32]{2,1,0:T(8,128)}, u32[]{:S(2)}) copy-start(f32[3,32,32]{2,1,0:T(8,128)} %param.13) | copy-start | bytes 36868
  222.4 4.4 %copy-start.5 = (pred[9,17,129]{2,1,0:T(8,128)(4,1)S(1)}, pred[9,17,129]{2,1,0:T(8,128)(4,1)}, u32[]{:S(2)}) copy-start(pred[9,17,129]{2,1,0:T(8,128)(4,1)} %broadcast_and_fusion) | copy-start | bytes 59215
  226.8 7.9 %copy-start.4 = (s32[8,16,128]{2,1,0:T(8,128)S(1)}, s32[8,16,128]{2,1,0:T(8,128)}, u32[]{:S(2)}) copy-start(s32[8,16,128]{2,1,0:T(8,128)} %sign.14) | copy-start | bytes 196612
  226.8 7.9 %copy-start.7 = (s32[4]{0:T(128)S(1)}, s32[4]{0:T(128)}, u32[]{:S(2)}) copy-start(s32[4]{0:T(128)} %get-tuple-element.85) | copy-start | bytes 52
  226.9 7.9 %copy-start.8 = (f32[4]{0:T(128)S(1)}, f32[4]{0:T(128)}, u32[]{:S(2)}) copy-start(f32[4]{0:T(128)} %compare_convert_fusion) | copy-start | bytes 52
where the time goes:
time: 244 us; the launch traced here: 241 us
  blocking collectives  112 us (46%)
  local copies, waits for them, and re-layouts  39.8 us (16%)
  starting transfers between devices  38.7 us (16%)
  other arithmetic  21.3 us (9%)
  matrix products  16.1 us (7%)
  waiting for transfers between devices  11.8 us (5%)
    pmax x1, blocking collectives, shards(): top_speed = lax.pmax(jnp.max(jnp.abs(flow_rate)), ('gx', 'gy', 'gz'))  112 us
    another operation x35, local copies, waits for them, and re-layouts, element_stiffness(): jnp.stack([corner(widened[2 + k], offset) for k in range(4) for offset in...  33.6 us
    ppermute x6, starting transfers between devices, with_halo(): lax.ppermute(tail, axis, [(i, (i + 1) % count) for i in range(ends)])  26.9 us
    ppermute x6, starting transfers between devices, with_halo(): lax.ppermute(head, axis, [((i + 1) % count, i) for i in range(ends)])  11.8 us
    ppermute x6, waiting for transfers between devices, with_halo(): lax.ppermute(head, axis, [((i + 1) % count, i) for i in range(ends)])  11.8 us
    dot_general x1, matrix products, element_stiffness(): jnp.einsum('ab,bxyz->axyz', local_operator_tiles[1], element_values, prec...  6.44 us
    select_n x1, other arithmetic, shards(): equation_misfit = jnp.where(fixed_dof, flow_guess, stiffness - source_term)  5.68 us
    dot_general x1, matrix products, element_stiffness(): jnp.einsum('ab,bxyz->axyz', local_operator_tiles[2], element_values, prec...  5.29 us
  transfers between devices with their start and end apart: 12, of which 3 were waited for; matrix products, arithmetic and copies ran while one was open for 4% of the time, Pallas kernels for 0%

commit v1 on v0

v1 whole, which is shorter than its diff:
```python
import functools

import jax
import jax.numpy as jnp
from jax import lax
from jax.experimental import pallas as pl
from jax.experimental.pallas import tpu as pltpu
from jax.sharding import PartitionSpec as P

MESH = pl.DeviceIdType.MESH
F32 = jnp.float32
BF16 = jnp.bfloat16

LX, LY, LZ = 8, 16, 128
NODES = LX * LY
EX, EY = LX + 2, LY + 2
CX, CY = LX + 1, LY + 1
TR = 32
PW = 256
COEF, TEMP, RATE = 4, 5, 6


def lanes(shape):
    return lax.broadcasted_iota(jnp.int32, shape, 1)


def exchange(
    sizes,
    rheo_in,
    ops_in,
    heat,
    rate,
    guess,
    rock,
    mask,
    nat,
    mk,
    f,
    f2,
    fp,
    sums,
    ce,
    ends,
    speed,
    rheo,
    ops,
    vel,
    rk,
    te,
    ge,
    sx,
    rx,
    sy,
    ry,
    se,
    re,
    stz,
    rtz,
    sp,
    rp,
    tops,
    xb,
    wts,
    lsem,
    ss,
    rs,
    ms,
    mr,
):
    nx, ny, nz = sizes
    gx, gy, gz = lax.axis_index("gx"), lax.axis_index("gy"), lax.axis_index("gz")
    has_x = (gx > 0, gx < nx - 1)
    has_y = (gy > 0, gy < ny - 1)
    has_z = (gz > 0, gz < nz - 1)

    barrier = pltpu.get_barrier_semaphore()

    stages = (
        (nx * ny, gy * nx + gx, lambda t: {"gx": lax.rem(t, nx), "gy": t // nx}),
        (nz, gz, lambda t: {"gz": t}),
    )
    step_x = ({"gx": gx - 1}, {"gx": gx + 1})
    step_y = ({"gy": gy - 1}, {"gy": gy + 1})
    step_z = ({"gz": gz - 1}, {"gz": gz + 1})
    step_e = [dict(**step_x[e // 2], **step_y[e % 2]) for e in range(4)]
    has_e = [jnp.logical_and(has_x[e // 2], has_y[e % 2]) for e in range(4)]

    def greet(device):
        pl.semaphore_signal(barrier, inc=1, device_id=device, device_id_type=MESH)

    def far_first(j, size):
        return 1 + lax.rem(j - 1 + size // 2, max(size - 1, 1))

    for size, own, at in stages:

        def greet_one(j, carry):
            greet(at(lax.rem(own + far_first(j, size), size)))
            return carry

        lax.fori_loop(1, size, greet_one, 0)

    locals_ = [
        pltpu.make_async_copy(rate, vel, lsem.at[0]),
        pltpu.make_async_copy(heat, nat.at[pl.ds(TEMP * NODES, NODES)], lsem.at[1]),
        pltpu.make_async_copy(guess, nat.at[pl.ds(0, 4 * NODES)], lsem.at[2]),
        pltpu.make_async_copy(rock, rk, lsem.at[3]),
        pltpu.make_async_copy(rheo_in, rheo, lsem.at[4]),
        pltpu.make_async_copy(ops_in, ops, lsem.at[5]),
        pltpu.make_async_copy(mask, mk, lsem.at[6]),
    ]
    for copy in locals_:
        copy.start()

    for d in range(2):

        @pl.when(jnp.logical_not(has_x[d]))
        def _():
            rx[d] = jnp.zeros((8 * LY, LZ), F32)
            rx[d, pl.ds(COEF * LY, LY), :] = jnp.ones((LY, LZ), F32)

        @pl.when(jnp.logical_not(has_y[d]))
        def _():
            ry[d] = jnp.zeros((8 * LX, LZ), F32)
            ry[d, pl.ds(COEF * LX, LX), :] = jnp.ones((LX, LZ), F32)

        @pl.when(jnp.logical_not(has_z[d]))
        def _():
            rtz[d] = jnp.zeros((8, LZ), F32)
            rp[d] = jnp.where(
                lax.broadcasted_iota(jnp.int32, (8, PW), 0) == COEF, 1.0, 0.0
            ).astype(F32)

    for e in range(4):

        @pl.when(jnp.logical_not(has_e[e]))
        def _():
            re[e] = jnp.where(
                lax.broadcasted_iota(jnp.int32, (8, LZ), 0) == COEF, 1.0, 0.0
            ).astype(F32)

    nat[pl.ds(7 * NODES, NODES), :] = jnp.zeros((NODES, LZ), F32)

    locals_[0].wait()
    top = jnp.abs(vel[pl.ds(0, 8), :])

    def top_step(i, top):
        for k in range(8):
            top = jnp.maximum(top, jnp.abs(vel[pl.ds(pl.multiple_of(i * 64 + k * 8, 8), 8), :]))
        return top

    top = lax.fori_loop(0, 3 * NODES // 64, top_step, top)
    tops[0, stages[0][1]] = jnp.max(top, axis=0, keepdims=True)

    locals_[1].wait()
    lane = lanes((8, LZ))
    t0 = TEMP * NODES
    for d in range(2):
        xs, ys = (0, LX - 1)[d], (0, LY - 1)[d]
        sx[d, pl.ds(TEMP * LY, LY), :] = nat[pl.ds(t0 + xs * LY, LY), :]
        sy[d, pl.ds(TEMP * LX, LX), :] = nat[pl.ds(t0 + ys, LX, stride=LY), :]
    low = jnp.zeros((8, LZ), F32)
    high = jnp.zeros((8, LZ), F32)
    for j in range(NODES // 8):
        r = nat[pl.ds(t0 + j * 8, 8), :]
        if j:
            r = pltpu.roll(r, j, 1)
        low = jnp.where(lane == j, r, low)
        high = jnp.where(lane == (j - 1) % LZ, r, high)
    stz[0] = low
    stz[1] = high

    locals_[2].wait()
    locals_[3].wait()
    locals_[4].wait()

    for i in range(NODES // 8):
        label = rk[pl.ds(i * 8, 8), :]
        total = jnp.zeros((8, LZ), F32)
        for k in range(4):
            total = total + jnp.where(label == k, rheo[k], 0.0)
        nat[pl.ds(COEF * NODES + i * 8, 8), :] = total
    for d in range(2):
        xs, ys = (0, LX - 1)[d], (0, LY - 1)[d]
        for k in range(5):
            sx[d, pl.ds(k * LY, LY), :] = nat[pl.ds(k * NODES + xs * LY, LY), :]
            sy[d, pl.ds(k * LX, LX), :] = nat[pl.ds(k * NODES + ys, LX, stride=LY), :]
    row = lax.broadcasted_iota(jnp.int32, (32, 32), 0)
    col = lax.broadcasted_iota(jnp.int32, (32, 32), 1)
    from_row = 8 * (row & 3) + 2 * (row >> 3) + ((row >> 2) & 1)
    pick_row = jnp.where(col == from_row, 1.0, 0.0).astype(BF16)
    row = lax.broadcasted_iota(jnp.int32, (32, 128), 0)
    col = lax.broadcasted_iota(jnp.int32, (32, 128), 1)
    from_col = 8 * (col & 3) + 2 * ((col >> 4) & 3) + ((col >> 2) & 1)
    pick_col = jnp.where(row == from_col, 1.0, 0.0).astype(BF16)
    locals_[5].wait()
    for m in range(3):
        block = ops[m]
        head = block.astype(BF16)
        tail = (block - head.astype(F32)).astype(BF16)
        parts = []
        for part in (head, tail):
            part = jnp.dot(pick_row, part, preferred_element_type=F32).astype(BF16)
            parts.append(jnp.dot(part, pick_col, preferred_element_type=F32))
        wts[pl.ds(32 * m, 32), :] = jnp.where(col < 64, parts[0], parts[1]).astype(BF16)

    upper = lax.broadcasted_iota(jnp.int32, (8, LZ), 0) < 4

    def put_column(at, tile):
        both = jnp.where(upper, tile, pltpu.roll(pltpu.roll(tile, LZ - 1, 1), 4, 0))
        head = both.astype(BF16).astype(F32)
        xb[at] = jnp.concatenate([head, both - head], axis=0).astype(BF16)

    def own_columns(x, carry):
        for y in range(LY):
            put_column((x + 1) * EY + y + 1, nat[pl.ds(x * LY + y, 8, stride=NODES), :])
        return carry

    lax.fori_loop(0, LX, own_columns, 0)

    pl.semaphore_wait(barrier, nx * ny - 1 + nz - 1)

    def top_send(i):
        size, own, at = stages[i]

        def one(j, carry):
            pltpu.make_async_remote_copy(
                src_ref=tops.at[i, own],
                dst_ref=tops.at[i, own],
                send_sem=ms.at[i],
                recv_sem=mr.at[i],
                device_id=at(lax.rem(own + far_first(j, size), size)),
                device_id_type=MESH,
            ).start()
            return carry

        lax.fori_loop(1, size, one, 0)

    def top_wait(i, sem):
        rows = tops.at[i, pl.ds(0, stages[i][0] - 1)]
        pltpu.make_async_copy(rows, rows, sem.at[i]).wait()

    def top_gather(i):
        top_wait(i, mr)
        return jnp.max(tops[i, pl.ds(0, stages[i][0])], axis=0)

    def top_pass(i):
        tops[i + 1, stages[i + 1][1]] = top_gather(i)
        top_send(i + 1)


    def halo(src, dst, first, opposite, count, device, d, recv, rows=None):
        slot = d if recv else opposite
        span = None if rows is None else rows[1 - d if recv else d]
        part = (lambda ref, i: ref.at[i]) if rows is None else (lambda ref, i: ref.at[i, pl.ds(*span)])
        return pltpu.make_async_remote_copy(
            src_ref=part(src, d),
            dst_ref=part(dst, slot),
            send_sem=ss.at[first + d],
            recv_sem=rs.at[first + slot],
            device_id=device,
            device_id_type=MESH,
        )

    def group(has, src, dst, first, devices, rows=None):
        count = len(has)
        return [
            (
                has[d],
                functools.partial(halo, src, dst, first, count - 1 - d, count, devices[d], d, False, rows),
                functools.partial(halo, src, dst, first, count - 1 - d, count, devices[d], d, True, rows),
            )
            for d in range(count)
        ]

    temp_x = group(has_x, sx, rx, 0, step_x, ((TEMP * LY, LY),) * 2)
    temp_y = group(has_y, sy, ry, 2, step_y, ((TEMP * LX, LX),) * 2)
    temp_z = group(has_z, stz, rtz, 4, step_z)
    state_x = group(has_x, sx, rx, 6, step_x, ((0, 4 * LY), (0, 5 * LY)))
    state_y = group(has_y, sy, ry, 8, step_y, ((0, 4 * LX), (0, 5 * LX)))
    rate_x = group(has_x, sx, rx, 10, step_x, ((RATE * LY, LY),) * 2)
    rate_y = group(has_y, sy, ry, 12, step_y, ((RATE * LX, LX),) * 2)
    edges = group(has_e, se, re, 14, step_e)
    planes = group(has_z, sp, rp, 18, step_z)

    def start(copies):
        for has, send, _ in copies:

            @pl.when(has)
            def _():
                send().start()

    def wait(copies):
        for has, _, recv in copies:

            @pl.when(has)
            def _():
                recv().wait_recv()

    def sent(copies):
        for has, send, _ in copies:

            @pl.when(has)
            def _():
                send().wait_send()

    start(temp_y + temp_x + temp_z)
    top_send(0)

    start(state_y + state_x)

    w = wts[...]

    def cell_matrix(x, y):
        a = xb[pl.ds(x * EY + y, 2)].reshape(32, LZ)
        b = xb[pl.ds((x + 1) * EY + y, 2)].reshape(32, LZ)
        return jnp.concatenate([a, b, a, b], axis=0)

    def middle(x, w):
        for y in range(1, LY, 2):
            pair = [cell_matrix(x, y)]
            if y + 1 < LY:
                pair.append(cell_matrix(x, y + 1))
            got = jnp.dot(w, jnp.concatenate(pair, axis=1), preferred_element_type=F32)
            for k in range(len(pair)):
                f[x * CY + y + k] = got[:, k * LZ : (k + 1) * LZ]

    def sides(x, present):
        pair = [
            jnp.where(jnp.logical_and(present, has_y[d]), cell_matrix(x, (0, LY)[d]), jnp.zeros((128, LZ), BF16))
            for d in range(2)
        ]
        got = jnp.dot(w, jnp.concatenate(pair, axis=1), preferred_element_type=F32)
        for k in range(2):
            f[x * CY + (0, LY)[k]] = got[:, k * LZ : (k + 1) * LZ]

    def inner_row(x, carry):
        middle(x, w)
        return carry

    lax.fori_loop(1, 5, inner_row, 0)

    wait(temp_y + temp_x + temp_z)

    def border(dst, field):
        for x in range(LX):
            dst[pl.ds((x + 1) * TR + 8, LY), :] = nat[pl.ds(field * NODES + x * LY, LY), :]

    def border_faces(dst, field, sides):
        for d in sides:
            dst[pl.ds((0, EX - 1)[d] * TR + 8, LY), :] = rx[d, pl.ds(field * LY, LY), :]
            dst[pl.ds(TR + (7, 8 + LY)[d], LX, stride=TR), :] = ry[d, pl.ds(field * LX, LX), :]

    def border_edges(dst, field, which):
        for e in which:
            at = (0, EX - 1)[e // 2] * TR + (7, 8 + LY)[e % 2]
            dst[pl.ds(at, 1), :] = re[e, pl.ds(field, 1), :]

    border(te, TEMP)
    border_faces(te, TEMP, (0, 1))
    for x in range(LX):
        for h in range(2):
            j = 2 * x + h
            at = (x + 1) * TR + 8 + 8 * h
            centre = te[pl.ds(at, 8), :]
            plus_x, minus_x = te[pl.ds(at + TR, 8), :], te[pl.ds(at - TR, 8), :]
            plus_y, minus_y = te[pl.ds(at + 1, 8), :], te[pl.ds(at - 1, 8), :]
            from_low = rtz[0] if j == 1 else pltpu.roll(rtz[0], (1 - j) % LZ, 1)
            from_high = pltpu.roll(rtz[1], LZ - 1 - j, 1)
            minus_z = jnp.where(lane == 0, from_low, pltpu.roll(centre, 1, 1))
            plus_z = jnp.where(lane == LZ - 1, from_high, pltpu.roll(centre, LZ - 1, 1))
            laplace = plus_x + minus_x + plus_y + minus_y + plus_z + minus_z - 6.0 * centre
            v = [vel[pl.ds(k * NODES + j * 8, 8), :] for k in range(3)]
            transport = (
                v[0] * (plus_x - minus_x) + v[1] * (plus_y - minus_y) + v[2] * (plus_z - minus_z)
            )
            nat[pl.ds(RATE * NODES + j * 8, 8), :] = laplace - 0.5 * transport
    r0 = RATE * NODES
    for d in range(2):
        xs, ys = (0, LX - 1)[d], (0, LY - 1)[d]
        sx[d, pl.ds(RATE * LY, LY), :] = nat[pl.ds(r0 + xs * LY, LY), :]
        sy[d, pl.ds(RATE * LX, LX), :] = nat[pl.ds(r0 + ys, LX, stride=LY), :]
    for e in range(4):
        at = (0, LX - 1)[e // 2] * LY + (0, LY - 1)[e % 2]
        se[e] = nat[pl.ds(at, 8, stride=NODES), :]
    start(rate_y + rate_x + edges)
    lax.fori_loop(5, LX, inner_row, 0)
    top_pass(0)

    def plane_row(tiles, first):
        low = jnp.zeros((8, LZ), F32)
        high = jnp.zeros((8, LZ), F32)
        for k, tile in enumerate(tiles):
            y = first + k
            r = pltpu.roll(tile, y, 1) if y else tile
            low = jnp.where(lane == y, r, low)
            high = jnp.where(lane == (y - 1) % LZ, r, high)
        return low, pltpu.roll(high, 1, 1)

    def add_plane(x, low, high):
        for i, part in enumerate((low, high)):
            wide = jnp.concatenate([part, jnp.zeros((8, PW - LZ), F32)], axis=1)
            sp[i] = sp[i] + pltpu.roll(wide, x * EY, 1)

    sp[...] = jnp.zeros((2, 8, PW), F32)

    def own_plane(x, carry):
        tiles = [nat[pl.ds(x * LY + y, 8, stride=NODES), :] for y in range(LY)]
        add_plane(x + 1, *plane_row(tiles, 1))
        return carry

    lax.fori_loop(0, LX, own_plane, 0)

    wait(state_y + state_x + rate_y + rate_x + edges)
    for d in range(2):
        x = (0, EX - 1)[d]
        tiles = [re[2 * d]]
        tiles += [rx[d, pl.ds(y, 8, stride=LY), :] for y in range(LY)]
        tiles += [re[2 * d + 1]]
        for y in range(EY):
            put_column(x * EY + y, tiles[y])
        add_plane(x, *plane_row(tiles, 0))

    def side_columns(x, carry):
        low_tile = ry[0, pl.ds(x, 8, stride=LX), :]
        high_tile = ry[1, pl.ds(x, 8, stride=LX), :]
        put_column((x + 1) * EY, low_tile)
        put_column((x + 1) * EY + EY - 1, high_tile)
        a = plane_row([low_tile], 0)
        b = plane_row([high_tile], EY - 1)
        add_plane(x + 1, a[0] + b[0], a[1] + b[1])
        return carry

    lax.fori_loop(0, LX, side_columns, 0)
    start(planes)

    for x in range(1, LX):
        sides(x, True)
    for d in range(2):
        x = (0, LX)[d]
        middle(x, jnp.where(has_x[d], w, jnp.zeros((96, 128), BF16)))
        sides(x, has_x[d])

    def rows_at(x, y, m, q):
        return f[(x + 1 - (q >> 1)) * CY + y + 1 - (q & 1), pl.ds(32 * m + 8 * q, 8), :]

    def fixed_row(x, carry):
        for y in range(LY):
            f2[x * LY + y] = sum(rows_at(x, y, 2, q) for q in range(4))
        return carry

    lax.fori_loop(0, LX, fixed_row, 0)

    border_edges(te, TEMP, range(4))
    border(ge, RATE)
    border_faces(ge, RATE, (0, 1))
    border_edges(ge, RATE, range(4))
    border(ce, COEF)
    border_faces(ce, COEF, (0,))
    border_edges(ce, COEF, (0,))

    for i, ref in enumerate((te, ge)):
        for x in range(CX):
            total = ref[pl.ds(x * TR, TR), :] + ref[pl.ds((x + 1) * TR, TR), :]
            total = total + pltpu.roll(total, LZ - 1, 1)
            total = total + pltpu.roll(total, TR - 1, 0)
            sums[i, x] = total[:24]

    wait(planes)

    def shifted(a, q, back):
        by = EY * (q >> 1) + (q & 1)
        by = by if back else (PW - by) % PW
        return pltpu.roll(a, by, 1) if by else a

    place = lanes((8, PW))
    place_x = (place * 3641) >> 16
    place_y = place - EY * place_x
    outside = jnp.logical_or(
        jnp.logical_or(
            jnp.logical_and(place_x == 0, jnp.logical_not(has_x[0])),
            jnp.logical_and(place_x == LX, jnp.logical_not(has_x[1])),
        ),
        jnp.logical_or(
            jnp.logical_and(place_y == 0, jnp.logical_not(has_y[0])),
            jnp.logical_and(place_y == LY, jnp.logical_not(has_y[1])),
        ),
    )
    upper_wide = lax.broadcasted_iota(jnp.int32, (8, PW), 0) < 4
    for i in range(2):
        below, above = (rp[0], sp[0]) if i == 0 else (sp[1], rp[1])
        both = jnp.where(upper_wide, below, pltpu.roll(above, 4, 0))
        both = jnp.where(has_z[i], both, jnp.zeros((8, PW), F32))
        columns = []
        for q in range(4):
            part = jnp.where(outside, 0.0, shifted(both, q, False))
            head = part.astype(BF16).astype(F32)
            columns.append(jnp.concatenate([head, part - head], axis=0).astype(BF16))
        fp[i] = jnp.dot(w, jnp.concatenate(columns + columns, axis=0), preferred_element_type=F32)
        total = below + above
        total = sum(shifted(total, q, False) for q in range(4))
        ends[i] = total
        ends[i, pl.ds(COEF, 1), :] = below[COEF : COEF + 1]

    speed[...] = jnp.broadcast_to(jnp.max(top_gather(1), axis=1, keepdims=True), (8, LZ))
    locals_[6].wait()

    for i in range(2):
        top_wait(i, ms)
    sent(temp_x + temp_y + temp_z + state_x + state_y + rate_x + rate_y + edges + planes)


def finish(
    nat,
    mk,
    f,
    f2,
    fp,
    sums,
    ce,
    ends,
    speed,
    out_t,
    out_r,
    vis,
    nod,
    zp,
    lat,
    res,
    osem,
):
    t0, r0 = TEMP * NODES, RATE * NODES
    lane = lanes((8, LZ))
    upper_wide = lax.broadcasted_iota(jnp.int32, (8, PW), 0) < 4

    def shifted(a, q, back):
        by = EY * (q >> 1) + (q & 1)
        by = by if back else (PW - by) % PW
        return pltpu.roll(a, by, 1) if by else a

    def rows_at(x, y, m, q):
        return f[(x + 1 - (q >> 1)) * CY + y + 1 - (q & 1), pl.ds(32 * m + 8 * q, 8), :]

    step = 0.5 / (speed[0:1, :] + 6.0)
    step_wide = 0.5 / (speed[0:1, 0:1] + 6.0)

    for j in range(NODES // 8):
        lat[pl.ds(j * 8, 8), :] = (
            nat[pl.ds(t0 + j * 8, 8), :] + step * nat[pl.ds(r0 + j * 8, 8), :]
        )

    put_t = pltpu.make_async_copy(lat, out_t, osem.at[0])
    put_t.start()
    for x in range(CX):
        total = sums[0, x] + step * sums[1, x]
        viscosity = ce[pl.ds(x * TR, 24), :] * jnp.exp(1.5 - 0.375 * total)
        vis[0, x] = viscosity
        vis[1, x] = 0.25 / viscosity

    forces = []
    for i in range(2):
        coefficient = ends[i, pl.ds(COEF, 1), :]
        temp, change = ends[i, pl.ds(TEMP, 1), :], ends[i, pl.ds(RATE, 1), :]
        viscosity = coefficient * jnp.exp(1.5 - 0.375 * (temp + step_wide * change))
        stabilize = 0.25 / viscosity
        forces.append(
            viscosity * fp[i, pl.ds(0, 32), :]
            + stabilize * fp[i, pl.ds(32, 32), :]
            + fp[i, pl.ds(64, 32), :]
        )
    last = sum(
        shifted(jnp.where(upper_wide, forces[1][8 * q : 8 * q + 8], forces[0][8 * q : 8 * q + 8]), q, True)
        for q in range(4)
    )
    zp[...] = last

    is_last = lane == LZ - 1

    def node_row(x, carry):
        ends_row = pltpu.roll(zp[...], PW - EY * (x + 1), 1)[:, :LZ]
        for y in range(LY):
            total = f2[x * LY + y]
            for q in range(4):
                cell_x, cell_y = x + 1 - (q >> 1), y + 1 - (q & 1)
                viscosity = vis[0, cell_x, pl.ds(7 + cell_y, 1), :]
                stabilize = vis[1, cell_x, pl.ds(7 + cell_y, 1), :]
                total = total + viscosity * rows_at(x, y, 0, q) + stabilize * rows_at(x, y, 1, q)
            total = jnp.where(is_last, pltpu.roll(ends_row, LZ - 2 - y, 1), total)
            nod[pl.ds(y * 8, 8), :] = total
        for h in range(2):
            at = pl.multiple_of(x * LY + 8 * h, 8)
            flags = mk[pl.ds(at, 8), :]
            for c in range(4):
                near = nod[pl.ds(64 * h + c, 8, stride=8), :]
                far = nod[pl.ds(64 * h + 4 + c, 8, stride=8), :]
                value = near + pltpu.roll(far, 1, 1)
                if c == 2:
                    value = value - 2.0 * lat[pl.ds(at, 8), :]
                state = nat[pl.ds(pl.multiple_of(c * NODES + at, 8), 8), :]
                res[c, pl.ds(at, 8), :] = jnp.where((flags & (1 << c)) != 0, state, value)
        return carry

    puts = [put_t]
    for h in range(2):
        lax.fori_loop(h * LX // 2, (h + 1) * LX // 2, node_row, 0)
        part = pl.ds(h * NODES // 2, NODES // 2)
        puts.append(pltpu.make_async_copy(res.at[:, part], out_r.at[:, part], osem.at[1 + h]))
        puts[-1].start()
    for put in puts:
        put.wait()


def solution(mesh):
    sizes = nx, ny, nz = tuple(mesh.shape[a] for a in ("gx", "gy", "gz"))
    vmem = pltpu.VMEM
    hbm_spec = pl.BlockSpec(memory_space=pltpu.HBM)
    vmem_spec = pl.BlockSpec(memory_space=vmem)

    def in_hbm(a):
        return pltpu.with_memory_space_constraint(a, pltpu.HBM)

    def shards(heat, rate, guess, rock, mask, rheo, ops):
        kept = pl.pallas_call(
            functools.partial(exchange, sizes),
            out_shape=(
                vmem((8 * NODES, LZ), F32),
                vmem((NODES, LZ), jnp.int32),
                vmem((CX * CY, 96, LZ), F32),
                vmem((NODES, 8, LZ), F32),
                vmem((2, 96, PW), F32),
                vmem((2, CX, 24, LZ), F32),
                vmem((EX * TR, LZ), F32),
                vmem((2, 8, PW), F32),
                vmem((8, LZ), F32),
            ),
            in_specs=[hbm_spec] * 7,
            out_specs=[vmem_spec] * 9,
            scratch_shapes=[
                pltpu.SMEM((4,), F32),
                vmem((3, 32, 32), F32),
                vmem((3 * NODES, LZ), F32),
                vmem((NODES, LZ), jnp.int32),
                vmem((EX * TR, LZ), F32),
                vmem((EX * TR, LZ), F32),
                vmem((2, 8 * LY, LZ), F32),
                vmem((2, 8 * LY, LZ), F32),
                vmem((2, 8 * LX, LZ), F32),
                vmem((2, 8 * LX, LZ), F32),
                vmem((4, 8, LZ), F32),
                vmem((4, 8, LZ), F32),
                vmem((2, 8, LZ), F32),
                vmem((2, 8, LZ), F32),
                vmem((2, 8, PW), F32),
                vmem((2, 8, PW), F32),
                vmem((2, max(nx * ny, nz), 1, LZ), F32),
                vmem((EX * EY, 16, LZ), BF16),
                vmem((96, 128), BF16),
                pltpu.SemaphoreType.DMA((7,)),
                pltpu.SemaphoreType.DMA((20,)),
                pltpu.SemaphoreType.DMA((20,)),
                pltpu.SemaphoreType.DMA((2,)),
                pltpu.SemaphoreType.DMA((2,)),
            ],
            compiler_params=pltpu.CompilerParams(
                collective_id=0, has_side_effects=True, vmem_limit_bytes=24 * 1024 * 1024
            ),
        )(
            in_hbm(rheo),
            in_hbm(ops),
            in_hbm(heat.reshape(NODES, LZ)),
            in_hbm(rate.reshape(3 * NODES, LZ)),
            in_hbm(guess.reshape(4 * NODES, LZ)),
            in_hbm(rock.reshape(NODES, LZ)),
            in_hbm(mask.reshape(NODES, LZ)),
        )
        out_t, out_r = pl.pallas_call(
            finish,
            out_shape=(pltpu.HBM((NODES, LZ), F32), pltpu.HBM((4, NODES, LZ), F32)),
            in_specs=[vmem_spec] * 9,
            out_specs=[hbm_spec] * 2,
            scratch_shapes=[
                vmem((2, CX, 24, LZ), F32),
                vmem((8 * LY, LZ), F32),
                vmem((8, PW), F32),
                vmem((NODES, LZ), F32),
                vmem((4, NODES, LZ), F32),
                pltpu.SemaphoreType.DMA((3,)),
            ],
            compiler_params=pltpu.CompilerParams(vmem_limit_bytes=24 * 1024 * 1024),
        )(*(pltpu.with_memory_space_constraint(a, vmem) for a in kept))
        return out_t.reshape(LX, LY, LZ), out_r.reshape(4, LX, LY, LZ)

    grid = P("gx", "gy", "gz")
    fields = P(None, "gx", "gy", "gz")
    return jax.shard_map(
        shards,
        mesh=mesh,
        in_specs=(grid, fields, fields, grid, grid, P(), P()),
        out_specs=(grid, fields),
        check_vma=False,
    )
```

time: 244 us -> 35.8 us (0.15); the launches traced: 241 us -> 35.6 us
  blocking collectives: 112 us -> 0 us
  local copies, waits for them, and re-layouts: 39.8 us -> 0 us
  starting transfers between devices: 38.7 us -> 0 us
  Pallas kernels: 0 us -> 35 us
  other arithmetic: 21.3 us -> 0 us
  matrix products: 16.1 us -> 0 us
  waiting for transfers between devices: 11.8 us -> 0 us
    pmax x1 -> x0, blocking collectives: 112 us -> none  [shards(): top_speed = lax.pmax(jnp.max(jnp.abs(flow_rate)), ('gx', 'gy', 'gz'))]
    ppermute x12 -> x0, starting transfers between devices: 38.7 us -> none  [the longest x6 26.9 us: with_halo(): lax.ppermute(tail, axis, [(i, (i + 1) % count) for i in range(ends)])]
    pallas_call x0 -> x2, Pallas kernels: none -> 35 us  [the longest x1 32.2 us: shards(): pl.pallas_call(functools.partial(exchange, sizes), out_shape=(vmem((8 * N...]
    another operation x35 -> x0, local copies, waits for them, and re-layouts: 33.6 us -> none  [element_stiffness(): jnp.stack([corner(widened[2 + k], offset) for k in range(4) for offset in...]
    dot_general x3 -> x0, matrix products: 16.1 us -> none  [the longest x1 6.44 us: element_stiffness(): jnp.einsum('ab,bxyz->axyz', local_operator_tiles[1], element_values, prec...]
    ppermute x12 -> x0, waiting for transfers between devices: 11.8 us -> none  [the longest x6 11.8 us: with_halo(): lax.ppermute(head, axis, [((i + 1) % count, i) for i in range(ends)])]
    select_n x2 -> x0, other arithmetic: 6.28 us -> none  [the longest x1 5.68 us: shards(): equation_misfit = jnp.where(fixed_dof, flow_guess, stiffness - source_term)]
    slice x7 -> x0, local copies, waits for them, and re-layouts: 3.49 us -> none  [the longest x1 1.47 us: lookup(): rheology_coefficient[selector]]
  transfers between devices with their start and end apart: 12 -> 0, of which waited for: 3 -> 0; matrix products, arithmetic and copies ran while one was open for 4% -> 0% of each run, Pallas kernels for 0% -> 0%
where the time goes in v1:
time: 35.8 us; the launch traced here: 35.6 us
  Pallas kernels  35 us (98%)
  between operations  0.64 us (2%)
    pallas_call x1, Pallas kernels, shards(): pl.pallas_call(functools.partial(exchange, sizes), out_shape=(vmem((8 * N...  32.2 us
    pallas_call x1, Pallas kernels, shards(): pl.pallas_call(finish, out_shape=(pltpu.HBM((NODES, LZ), F32), pltpu.HBM(...  2.83 us

profile of v1, /device:TPU:1, one launch (start us, length us, event | category | flops | bytes accessed | tf_op | source)
XLA Modules:
  0.0 35.6 jit_solution(10790124727763738603)
XLA Ops:
  0.6 32.2 %shard_map.86 = (f32[1024,128]{1,0:T(8,128)S(1)}, s32[128,128]{1,0:T(8,128)S(1)}, f32[153,96,128]{2,1,0:T(8,128)S(1)}, f32[128,8,128]{2,1,0:T(8,128)S(1)}, f32[2...) custom-call(f32[4]{0:T(128)} %rheo_in.1, ...), custom_call_target="tpu_custom_call" | custom-call | tf_op jit(solution)/shard_map/pallas_call | solution.py:622
  32.8 2.8 %shard_map.87 = (f32[128,128]{1,0:T(8,128)}, f32[4,128,128]{2,1,0:T(8,128)}) custom-call(f32[1024,128]{1,0:T(8,128)S(1)} %get-tuple-element.13.nat, s32[128,128]{1,0:T(8,128)S(1)} %get-tuple-element.14.mk, f32[153,96,128]{2,1,0:T(8,128)S(1)} %get-tuple-element.15.f, f32[128,8,128]{2,1,0:T(8,128)S(1)} %get-tuple-element.16.f2, ...), custom_call_target="tpu_custom_call" | custom-call | tf_op jit(solution)/shard_map/pallas_call | solution.py:675

commit v2 on v1

--- a/solution.py
+++ b/solution.py
@@ -184,6 +184,97 @@
         for k in range(5):
             sx[d, pl.ds(k * LY, LY), :] = nat[pl.ds(k * NODES + xs * LY, LY), :]
             sy[d, pl.ds(k * LX, LX), :] = nat[pl.ds(k * NODES + ys, LX, stride=LY), :]
+    pl.semaphore_wait(barrier, nx * ny - 1 + nz - 1)
+
+    def top_send(i):
+        size, own, at = stages[i]
+
+        def one(j, carry):
+            pltpu.make_async_remote_copy(
+                src_ref=tops.at[i, own],
+                dst_ref=tops.at[i, own],
+                send_sem=ms.at[i],
+                recv_sem=mr.at[i],
+                device_id=at(lax.rem(own + far_first(j, size), size)),
+                device_id_type=MESH,
+            ).start()
+            return carry
+
+        lax.fori_loop(1, size, one, 0)
+
+    def top_wait(i, sem):
+        rows = tops.at[i, pl.ds(0, stages[i][0] - 1)]
+        pltpu.make_async_copy(rows, rows, sem.at[i]).wait()
+
+    def top_gather(i):
+        top_wait(i, mr)
+        return jnp.max(tops[i, pl.ds(0, stages[i][0])], axis=0)
+
+    def top_pass(i):
+        tops[i + 1, stages[i + 1][1]] = top_gather(i)
+        top_send(i + 1)
+
+
+    def halo(src, dst, first, opposite, count, device, d, recv, rows=None):
+        slot = d if recv else opposite
+        span = None if rows is None else rows[1 - d if recv else d]
+        part = (lambda ref, i: ref.at[i]) if rows is None else (lambda ref, i: ref.at[i, pl.ds(*span)])
+        return pltpu.make_async_remote_copy(
+            src_ref=part(src, d),
+            dst_ref=part(dst, slot),
+            send_sem=ss.at[first + d],
+            recv_sem=rs.at[first + slot],
+            device_id=device,
+            device_id_type=MESH,
+        )
+
+    def group(has, src, dst, first, devices, rows=None):
+        count = len(has)
+        return [
+            (
+                has[d],
+                functools.partial(halo, src, dst, first, count - 1 - d, count, devices[d], d, False, rows),
+                functools.partial(halo, src, dst, first, count - 1 - d, count, devices[d], d, True, rows),
+            )
+            for d in range(count)
+        ]
+
+    temp_x = group(has_x, sx, rx, 0, step_x, ((TEMP * LY, LY),) * 2)
+    temp_y = group(has_y, sy, ry, 2, step_y, ((TEMP * LX, LX),) * 2)
+    temp_z = group(has_z, stz, rtz, 4, step_z)
+    state_x = group(has_x, sx, rx, 6, step_x, ((0, 4 * LY), (0, 5 * LY)))
+    state_y = group(has_y, sy, ry, 8, step_y, ((0, 4 * LX), (0, 5 * LX)))
+    rate_x = group(has_x, sx, rx, 10, step_x, ((RATE * LY, LY),) * 2)
+    rate_y = group(has_y, sy, ry, 12, step_y, ((RATE * LX, LX),) * 2)
+    edges = group(has_e, se, re, 14, step_e)
+    planes = group(has_z, sp, rp, 18, step_z)
+
+    def start(copies):
+        for has, send, _ in copies:
+
+            @pl.when(has)
+            def _():
+                send().start()
+
+    def wait(copies):
+        for has, _, recv in copies:
+
+            @pl.when(has)
+            def _():
+                recv().wait_recv()
+
+    def sent(copies):
+        for has, send, _ in copies:
+
+            @pl.when(has)
+            def _():
+                send().wait_send()
+
+    start(temp_y + temp_x + temp_z)
+    top_send(0)
+
+    start(state_y + state_x)
+
     row = lax.broadcasted_iota(jnp.int32, (32, 32), 0)
     col = lax.broadcasted_iota(jnp.int32, (32, 32), 1)
     from_row = 8 * (row & 3) + 2 * (row >> 3) + ((row >> 2) & 1)
@@ -217,97 +308,6 @@
 
     lax.fori_loop(0, LX, own_columns, 0)
 
-    pl.semaphore_wait(barrier, nx * ny - 1 + nz - 1)
-
-    def top_send(i):
-        size, own, at = stages[i]
-
-        def one(j, carry):
-            pltpu.make_async_remote_copy(
-                src_ref=tops.at[i, own],
-                dst_ref=tops.at[i, own],
-                send_sem=ms.at[i],
-                recv_sem=mr.at[i],
-                device_id=at(lax.rem(own + far_first(j, size), size)),
-                device_id_type=MESH,
-            ).start()
-            return carry
-
-        lax.fori_loop(1, size, one, 0)
-
-    def top_wait(i, sem):
-        rows = tops.at[i, pl.ds(0, stages[i][0] - 1)]
-        pltpu.make_async_copy(rows, rows, sem.at[i]).wait()
-
-    def top_gather(i):
-        top_wait(i, mr)
-        return jnp.max(tops[i, pl.ds(0, stages[i][0])], axis=0)
-
-    def top_pass(i):
-        tops[i + 1, stages[i + 1][1]] = top_gather(i)
-        top_send(i + 1)
-
-
-    def halo(src, dst, first, opposite, count, device, d, recv, rows=None):
-        slot = d if recv else opposite
-        span = None if rows is None else rows[1 - d if recv else d]
-        part = (lambda ref, i: ref.at[i]) if rows is None else (lambda ref, i: ref.at[i, pl.ds(*span)])
-        return pltpu.make_async_remote_copy(
-            src_ref=part(src, d),
-            dst_ref=part(dst, slot),
-            send_sem=ss.at[first + d],
-            recv_sem=rs.at[first + slot],
-            device_id=device,
-            device_id_type=MESH,
-        )
-
-    def group(has, src, dst, first, devices, rows=None):
-        count = len(has)
-        return [
-            (
-                has[d],
-                functools.partial(halo, src, dst, first, count - 1 - d, count, devices[d], d, False, rows),
-                functools.partial(halo, src, dst, first, count - 1 - d, count, devices[d], d, True, rows),
-            )
-            for d in range(count)
-        ]
-
-    temp_x = group(has_x, sx, rx, 0, step_x, ((TEMP * LY, LY),) * 2)
-    temp_y = group(has_y, sy, ry, 2, step_y, ((TEMP * LX, LX),) * 2)
-    temp_z = group(has_z, stz, rtz, 4, step_z)
-    state_x = group(has_x, sx, rx, 6, step_x, ((0, 4 * LY), (0, 5 * LY)))
-    state_y = group(has_y, sy, ry, 8, step_y, ((0, 4 * LX), (0, 5 * LX)))
-    rate_x = group(has_x, sx, rx, 10, step_x, ((RATE * LY, LY),) * 2)
-    rate_y = group(has_y, sy, ry, 12, step_y, ((RATE * LX, LX),) * 2)
-    edges = group(has_e, se, re, 14, step_e)
-    planes = group(has_z, sp, rp, 18, step_z)
-
-    def start(copies):
-        for has, send, _ in copies:
-
-            @pl.when(has)
-            def _():
-                send().start()
-
-    def wait(copies):
-        for has, _, recv in copies:
-
-            @pl.when(has)
-            def _():
-                recv().wait_recv()
-
-    def sent(copies):
-        for has, send, _ in copies:
-
-            @pl.when(has)
-            def _():
-                send().wait_send()
-
-    start(temp_y + temp_x + temp_z)
-    top_send(0)
-
-    start(state_y + state_x)
-
     w = wts[...]
 
     def cell_matrix(x, y):
@@ -337,7 +337,7 @@
         middle(x, w)
         return carry
 
-    lax.fori_loop(1, 5, inner_row, 0)
+    lax.fori_loop(1, 3, inner_row, 0)
 
     wait(temp_y + temp_x + temp_z)
 
@@ -382,8 +382,8 @@
     for e in range(4):
         at = (0, LX - 1)[e // 2] * LY + (0, LY - 1)[e % 2]
         se[e] = nat[pl.ds(at, 8, stride=NODES), :]
-    start(rate_y + rate_x + edges)
-    lax.fori_loop(5, LX, inner_row, 0)
+    start(rate_y + edges + rate_x)
+    lax.fori_loop(3, LX, inner_row, 0)
     top_pass(0)
 
     def plane_row(tiles, first):
@@ -411,27 +411,33 @@
     lax.fori_loop(0, LX, own_plane, 0)
 
     wait(state_y + state_x + rate_y + rate_x + edges)
+    ring = []
     for d in range(2):
         x = (0, EX - 1)[d]
-        tiles = [re[2 * d]]
-        tiles += [rx[d, pl.ds(y, 8, stride=LY), :] for y in range(LY)]
-        tiles += [re[2 * d + 1]]
-        for y in range(EY):
-            put_column(x * EY + y, tiles[y])
-        add_plane(x, *plane_row(tiles, 0))
-
-    def side_columns(x, carry):
-        low_tile = ry[0, pl.ds(x, 8, stride=LX), :]
-        high_tile = ry[1, pl.ds(x, 8, stride=LX), :]
-        put_column((x + 1) * EY, low_tile)
-        put_column((x + 1) * EY + EY - 1, high_tile)
-        a = plane_row([low_tile], 0)
-        b = plane_row([high_tile], EY - 1)
-        add_plane(x + 1, a[0] + b[0], a[1] + b[1])
-        return carry
-
-    lax.fori_loop(0, LX, side_columns, 0)
+        ring.append((x, 0, functools.partial(lambda e: re[e], 2 * d)))
+        for y in range(LY):
+            ring.append((x, y + 1, functools.partial(lambda d, y: rx[d, pl.ds(y, 8, stride=LY), :], d, y)))
+        ring.append((x, EY - 1, functools.partial(lambda e: re[e], 2 * d + 1)))
+    for x in range(LX):
+        for d in range(2):
+            ring.append(
+                (x + 1, (0, EY - 1)[d], functools.partial(lambda d, x: ry[d, pl.ds(x, 8, stride=LX), :], d, x))
+            )
+    halves = [[jnp.zeros((8, LZ), F32) for _ in range(PW // LZ)] for _ in range(2)]
+    for x, y, tile in ring:
+        at = x * EY + y
+        r = tile()
+        if at % LZ:
+            r = pltpu.roll(r, at % LZ, 1)
+        for i in range(2):
+            to = (at - i) % PW
+            halves[i][to // LZ] = jnp.where(lane == to % LZ, r, halves[i][to // LZ])
+    sp[0] = sp[0] + jnp.concatenate(halves[0], axis=1)
+    sp[1] = sp[1] + pltpu.roll(jnp.concatenate(halves[1], axis=1), 1, 1)
     start(planes)
+
+    for x, y, tile in ring:
+        put_column(x * EY + y, tile())
 
     for x in range(1, LX):
         sides(x, True)
@@ -465,6 +471,8 @@
             total = total + pltpu.roll(total, TR - 1, 0)
             sums[i, x] = total[:24]
 
+    top_wait(0, ms)
+    sent(temp_x + temp_y + temp_z + state_x + state_y + rate_x + rate_y + edges)
     wait(planes)
 
     def shifted(a, q, back):
@@ -504,9 +512,8 @@
     speed[...] = jnp.broadcast_to(jnp.max(top_gather(1), axis=1, keepdims=True), (8, LZ))
     locals_[6].wait()
 
-    for i in range(2):
-        top_wait(i, ms)
-    sent(temp_x + temp_y + temp_z + state_x + state_y + rate_x + rate_y + edges + planes)
+    top_wait(1, ms)
+    sent(planes)
 
 
 def finish(

time: 35.8 us -> 34.1 us (0.953)
  Pallas kernels: 35 us -> 33.3 us
    pallas_call x1, Pallas kernels: 32.2 us -> 30.5 us  [shards(): pl.pallas_call(functools.partial(exchange, sizes), out_shape=(vmem((8 * N...]
where the time goes in v2:
time: 34.1 us; the launch traced here: 33.9 us
  Pallas kernels  33.3 us (98%)
  between operations  0.64 us (2%)
    pallas_call x1, Pallas kernels, shards(): pl.pallas_call(functools.partial(exchange, sizes), out_shape=(vmem((8 * N...  30.5 us
    pallas_call x1, Pallas kernels, shards(): pl.pallas_call(finish, out_shape=(pltpu.HBM((NODES, LZ), F32), pltpu.HBM(...  2.83 us

profile of v2, /device:TPU:1, one launch (start us, length us, event | category | flops | bytes accessed | tf_op | source)
XLA Modules:
  0.0 33.9 jit_solution(239687605975508876)
XLA Ops:
  0.6 30.5 %shard_map.86 = (f32[1024,128]{1,0:T(8,128)S(1)}, s32[128,128]{1,0:T(8,128)S(1)}, f32[153,96,128]{2,1,0:T(8,128)S(1)}, f32[128,8,128]{2,1,0:T(8,128)S(1)}, f32[2...) custom-call(f32[4]{0:T(128)} %rheo_in.1, ...), custom_call_target="tpu_custom_call" | custom-call | tf_op jit(solution)/shard_map/pallas_call | solution.py:629
  31.1 2.8 %shard_map.87 = (f32[128,128]{1,0:T(8,128)}, f32[4,128,128]{2,1,0:T(8,128)}) custom-call(f32[1024,128]{1,0:T(8,128)S(1)} %get-tuple-element.13.nat, s32[128,128]{1,0:T(8,128)S(1)} %get-tuple-element.14.mk, f32[153,96,128]{2,1,0:T(8,128)S(1)} %get-tuple-element.15.f, f32[128,8,128]{2,1,0:T(8,128)S(1)} %get-tuple-element.16.f2, ...), custom_call_target="tpu_custom_call" | custom-call | tf_op jit(solution)/shard_map/pallas_call | solution.py:682

commit v3 on v2

--- a/solution.py
+++ b/solution.py
@@ -54,6 +54,8 @@
     ry,
     se,
     re,
+    rgx,
+    rgy,
     stz,
     rtz,
     sp,
@@ -73,6 +75,18 @@
     has_y = (gy > 0, gy < ny - 1)
     has_z = (gz > 0, gz < nz - 1)
 
+    locals_ = [
+        pltpu.make_async_copy(rate, vel, lsem.at[0]),
+        pltpu.make_async_copy(heat, nat.at[pl.ds(TEMP * NODES, NODES)], lsem.at[1]),
+        pltpu.make_async_copy(guess, nat.at[pl.ds(0, 4 * NODES)], lsem.at[2]),
+        pltpu.make_async_copy(rock, rk, lsem.at[3]),
+        pltpu.make_async_copy(rheo_in, rheo, lsem.at[4]),
+        pltpu.make_async_copy(ops_in, ops, lsem.at[5]),
+        pltpu.make_async_copy(mask, mk, lsem.at[6]),
+    ]
+    for copy in locals_[:2]:
+        copy.start()
+
     barrier = pltpu.get_barrier_semaphore()
 
     stages = (
@@ -99,16 +113,7 @@
 
         lax.fori_loop(1, size, greet_one, 0)
 
-    locals_ = [
-        pltpu.make_async_copy(rate, vel, lsem.at[0]),
-        pltpu.make_async_copy(heat, nat.at[pl.ds(TEMP * NODES, NODES)], lsem.at[1]),
-        pltpu.make_async_copy(guess, nat.at[pl.ds(0, 4 * NODES)], lsem.at[2]),
-        pltpu.make_async_copy(rock, rk, lsem.at[3]),
-        pltpu.make_async_copy(rheo_in, rheo, lsem.at[4]),
-        pltpu.make_async_copy(ops_in, ops, lsem.at[5]),
-        pltpu.make_async_copy(mask, mk, lsem.at[6]),
-    ]
-    for copy in locals_:
+    for copy in locals_[2:]:
         copy.start()
 
     for d in range(2):
@@ -116,11 +121,13 @@
         @pl.when(jnp.logical_not(has_x[d]))
         def _():
             rx[d] = jnp.zeros((8 * LY, LZ), F32)
+            rgx[d] = jnp.zeros((LY, LZ), F32)
             rx[d, pl.ds(COEF * LY, LY), :] = jnp.ones((LY, LZ), F32)
 
         @pl.when(jnp.logical_not(has_y[d]))
         def _():
             ry[d] = jnp.zeros((8 * LX, LZ), F32)
+            rgy[d] = jnp.zeros((LX, LZ), F32)
             ry[d, pl.ds(COEF * LX, LX), :] = jnp.ones((LX, LZ), F32)
 
         @pl.when(jnp.logical_not(has_z[d]))
@@ -215,26 +222,29 @@
         top_send(i + 1)
 
 
-    def halo(src, dst, first, opposite, count, device, d, recv, rows=None):
+    def halo(src, dst, first, opposite, count, device, d, recv, rows=None, whole=False):
         slot = d if recv else opposite
         span = None if rows is None else rows[1 - d if recv else d]
-        part = (lambda ref, i: ref.at[i]) if rows is None else (lambda ref, i: ref.at[i, pl.ds(*span)])
+
+        def part(ref, i, whole):
+            return ref.at[i] if whole else ref.at[i, pl.ds(*span)]
+
         return pltpu.make_async_remote_copy(
-            src_ref=part(src, d),
-            dst_ref=part(dst, slot),
+            src_ref=part(src, d, rows is None),
+            dst_ref=part(dst, slot, rows is None or whole),
             send_sem=ss.at[first + d],
             recv_sem=rs.at[first + slot],
             device_id=device,
             device_id_type=MESH,
         )
 
-    def group(has, src, dst, first, devices, rows=None):
+    def group(has, src, dst, first, devices, rows=None, whole=False):
         count = len(has)
         return [
             (
                 has[d],
-                functools.partial(halo, src, dst, first, count - 1 - d, count, devices[d], d, False, rows),
-                functools.partial(halo, src, dst, first, count - 1 - d, count, devices[d], d, True, rows),
+                functools.partial(halo, src, dst, first, count - 1 - d, count, devices[d], d, False, rows, whole),
+                functools.partial(halo, src, dst, first, count - 1 - d, count, devices[d], d, True, rows, whole),
             )
             for d in range(count)
         ]
@@ -244,8 +254,8 @@
     temp_z = group(has_z, stz, rtz, 4, step_z)
     state_x = group(has_x, sx, rx, 6, step_x, ((0, 4 * LY), (0, 5 * LY)))
     state_y = group(has_y, sy, ry, 8, step_y, ((0, 4 * LX), (0, 5 * LX)))
-    rate_x = group(has_x, sx, rx, 10, step_x, ((RATE * LY, LY),) * 2)
-    rate_y = group(has_y, sy, ry, 12, step_y, ((RATE * LX, LX),) * 2)
+    rate_x = group(has_x, sx, rgx, 10, step_x, ((RATE * LY, LY),) * 2, True)
+    rate_y = group(has_y, sy, rgy, 12, step_y, ((RATE * LX, LX),) * 2, True)
     edges = group(has_e, se, re, 14, step_e)
     planes = group(has_z, sp, rp, 18, step_z)
 
@@ -383,8 +393,9 @@
         at = (0, LX - 1)[e // 2] * LY + (0, LY - 1)[e % 2]
         se[e] = nat[pl.ds(at, 8, stride=NODES), :]
     start(rate_y + edges + rate_x)
-    lax.fori_loop(3, LX, inner_row, 0)
+    lax.fori_loop(3, 5, inner_row, 0)
     top_pass(0)
+    lax.fori_loop(5, LX, inner_row, 0)
 
     def plane_row(tiles, first):
         low = jnp.zeros((8, LZ), F32)
@@ -410,19 +421,41 @@
 
     lax.fori_loop(0, LX, own_plane, 0)
 
-    wait(state_y + state_x + rate_y + rate_x + edges)
     ring = []
     for d in range(2):
-        x = (0, EX - 1)[d]
-        ring.append((x, 0, functools.partial(lambda e: re[e], 2 * d)))
         for y in range(LY):
-            ring.append((x, y + 1, functools.partial(lambda d, y: rx[d, pl.ds(y, 8, stride=LY), :], d, y)))
-        ring.append((x, EY - 1, functools.partial(lambda e: re[e], 2 * d + 1)))
-    for x in range(LX):
-        for d in range(2):
+            ring.append(
+                ((0, EX - 1)[d], y + 1, functools.partial(lambda d, y: rx[d, pl.ds(y, 8, stride=LY), :], d, y))
+            )
+        for x in range(LX):
             ring.append(
                 (x + 1, (0, EY - 1)[d], functools.partial(lambda d, x: ry[d, pl.ds(x, 8, stride=LX), :], d, x))
             )
+    for e in range(4):
+        ring.append(((0, EX - 1)[e // 2], (0, EY - 1)[e % 2], functools.partial(lambda e: re[e], e)))
+
+    wait(state_y + state_x)
+    for x, y, tile in ring[:-4]:
+        put_column(x * EY + y, tile())
+    for x in range(1, LX):
+        sides(x, True)
+    for d in range(2):
+        middle((0, LX)[d], jnp.where(has_x[d], w, jnp.zeros((96, 128), BF16)))
+
+    def rows_at(x, y, m, q):
+        return f[(x + 1 - (q >> 1)) * CY + y + 1 - (q & 1), pl.ds(32 * m + 8 * q, 8), :]
+
+    def fixed_row(x, carry):
+        for y in range(LY):
+            f2[x * LY + y] = sum(rows_at(x, y, 2, q) for q in range(4))
+        return carry
+
+    lax.fori_loop(1, LX - 1, fixed_row, 0)
+
+    wait(rate_y + rate_x + edges)
+    for d in range(2):
+        rx[d, pl.ds(RATE * LY, LY), :] = rgx[d]
+        ry[d, pl.ds(RATE * LX, LX), :] = rgy[d]
     halves = [[jnp.zeros((8, LZ), F32) for _ in range(PW // LZ)] for _ in range(2)]
     for x, y, tile in ring:
         at = x * EY + y
@@ -436,25 +469,12 @@
     sp[1] = sp[1] + pltpu.roll(jnp.concatenate(halves[1], axis=1), 1, 1)
     start(planes)
 
-    for x, y, tile in ring:
+    for x, y, tile in ring[-4:]:
         put_column(x * EY + y, tile())
-
-    for x in range(1, LX):
-        sides(x, True)
     for d in range(2):
-        x = (0, LX)[d]
-        middle(x, jnp.where(has_x[d], w, jnp.zeros((96, 128), BF16)))
-        sides(x, has_x[d])
-
-    def rows_at(x, y, m, q):
-        return f[(x + 1 - (q >> 1)) * CY + y + 1 - (q & 1), pl.ds(32 * m + 8 * q, 8), :]
-
-    def fixed_row(x, carry):
-        for y in range(LY):
-            f2[x * LY + y] = sum(rows_at(x, y, 2, q) for q in range(4))
-        return carry
-
-    lax.fori_loop(0, LX, fixed_row, 0)
+        sides((0, LX)[d], has_x[d])
+    for x in (0, LX - 1):
+        fixed_row(x, 0)
 
     border_edges(te, TEMP, range(4))
     border(ge, RATE)
@@ -654,6 +674,8 @@
                 vmem((2, 8 * LX, LZ), F32),
                 vmem((4, 8, LZ), F32),
                 vmem((4, 8, LZ), F32),
+                vmem((2, LY, LZ), F32),
+                vmem((2, LX, LZ), F32),
                 vmem((2, 8, LZ), F32),
                 vmem((2, 8, LZ), F32),
                 vmem((2, 8, PW), F32),

time: 34.1 us -> 35.4 us (1.038)
  Pallas kernels: 33.3 us -> 34.7 us
    pallas_call x1, Pallas kernels: 30.5 us -> 31.8 us  [shards(): pl.pallas_call(functools.partial(exchange, sizes), out_shape=(vmem((8 * N...]
where the time goes in v3:
time: 35.4 us; the launch traced here: 35.3 us
  Pallas kernels  34.7 us (98%)
  between operations  0.64 us (2%)
    pallas_call x1, Pallas kernels, shards(): pl.pallas_call(functools.partial(exchange, sizes), out_shape=(vmem((8 * N...  31.8 us
    pallas_call x1, Pallas kernels, shards(): pl.pallas_call(finish, out_shape=(pltpu.HBM((NODES, LZ), F32), pltpu.HBM(...  2.83 us

profile of v3, /device:TPU:1, one launch (start us, length us, event | category | flops | bytes accessed | tf_op | source)
XLA Modules:
  0.0 35.3 jit_solution(15363361516242909940)
XLA Ops:
  0.6 31.8 %shard_map.86 = (f32[1024,128]{1,0:T(8,128)S(1)}, s32[128,128]{1,0:T(8,128)S(1)}, f32[153,96,128]{2,1,0:T(8,128)S(1)}, f32[128,8,128]{2,1,0:T(8,128)S(1)}, f32[2...) custom-call(f32[4]{0:T(128)} %rheo_in.1, ...), custom_call_target="tpu_custom_call" | custom-call | tf_op jit(solution)/shard_map/pallas_call | solution.py:649
  32.5 2.8 %shard_map.87 = (f32[128,128]{1,0:T(8,128)}, f32[4,128,128]{2,1,0:T(8,128)}) custom-call(f32[1024,128]{1,0:T(8,128)S(1)} %get-tuple-element.13.nat, s32[128,128]{1,0:T(8,128)S(1)} %get-tuple-element.14.mk, f32[153,96,128]{2,1,0:T(8,128)S(1)} %get-tuple-element.15.f, f32[128,8,128]{2,1,0:T(8,128)S(1)} %get-tuple-element.16.f2, ...), custom_call_target="tpu_custom_call" | custom-call | tf_op jit(solution)/shard_map/pallas_call | solution.py:704

commit v4 on v3

--- a/solution.py
+++ b/solution.py
@@ -89,9 +89,12 @@
 
     barrier = pltpu.get_barrier_semaphore()
 
+    inner = min(nz, 8)
+    gz_in, gz_out = lax.rem(gz, inner), gz // inner
     stages = (
         (nx * ny, gy * nx + gx, lambda t: {"gx": lax.rem(t, nx), "gy": t // nx}),
-        (nz, gz, lambda t: {"gz": t}),
+        (nz // inner, gz_out, lambda t: {"gz": t * inner + gz_in}),
+        (inner, gz_in, lambda t: {"gz": gz_out * inner + t}),
     )
     step_x = ({"gx": gx - 1}, {"gx": gx + 1})
     step_y = ({"gy": gy - 1}, {"gy": gy + 1})
@@ -112,6 +115,15 @@
             return carry
 
         lax.fori_loop(1, size, greet_one, 0)
+
+    greeted = sum(size - 1 for size, _, _ in stages)
+    for d in range(2):
+
+        @pl.when(has_z[d])
+        def _():
+            greet(step_z[d])
+
+        greeted = greeted + has_z[d].astype(jnp.int32)
 
     for copy in locals_[2:]:
         copy.start()
@@ -176,22 +188,7 @@
     stz[0] = low
     stz[1] = high
 
-    locals_[2].wait()
-    locals_[3].wait()
-    locals_[4].wait()
-
-    for i in range(NODES // 8):
-        label = rk[pl.ds(i * 8, 8), :]
-        total = jnp.zeros((8, LZ), F32)
-        for k in range(4):
-            total = total + jnp.where(label == k, rheo[k], 0.0)
-        nat[pl.ds(COEF * NODES + i * 8, 8), :] = total
-    for d in range(2):
-        xs, ys = (0, LX - 1)[d], (0, LY - 1)[d]
-        for k in range(5):
-            sx[d, pl.ds(k * LY, LY), :] = nat[pl.ds(k * NODES + xs * LY, LY), :]
-            sy[d, pl.ds(k * LX, LX), :] = nat[pl.ds(k * NODES + ys, LX, stride=LY), :]
-    pl.semaphore_wait(barrier, nx * ny - 1 + nz - 1)
+    pl.semaphore_wait(barrier, greeted)
 
     def top_send(i):
         size, own, at = stages[i]
@@ -210,8 +207,9 @@
         lax.fori_loop(1, size, one, 0)
 
     def top_wait(i, sem):
-        rows = tops.at[i, pl.ds(0, stages[i][0] - 1)]
-        pltpu.make_async_copy(rows, rows, sem.at[i]).wait()
+        if stages[i][0] > 1:
+            rows = tops.at[i, pl.ds(0, stages[i][0] - 1)]
+            pltpu.make_async_copy(rows, rows, sem.at[i]).wait()
 
     def top_gather(i):
         top_wait(i, mr)
@@ -280,8 +278,24 @@
             def _():
                 send().wait_send()
 
+    top_send(0)
     start(temp_y + temp_x + temp_z)
-    top_send(0)
+
+    locals_[2].wait()
+    locals_[3].wait()
+    locals_[4].wait()
+
+    for i in range(NODES // 8):
+        label = rk[pl.ds(i * 8, 8), :]
+        total = jnp.zeros((8, LZ), F32)
+        for k in range(4):
+            total = total + jnp.where(label == k, rheo[k], 0.0)
+        nat[pl.ds(COEF * NODES + i * 8, 8), :] = total
+    for d in range(2):
+        xs, ys = (0, LX - 1)[d], (0, LY - 1)[d]
+        for k in range(5):
+            sx[d, pl.ds(k * LY, LY), :] = nat[pl.ds(k * NODES + xs * LY, LY), :]
+            sy[d, pl.ds(k * LX, LX), :] = nat[pl.ds(k * NODES + ys, LX, stride=LY), :]
 
     start(state_y + state_x)
 
@@ -420,6 +434,7 @@
         return carry
 
     lax.fori_loop(0, LX, own_plane, 0)
+    top_pass(1)
 
     ring = []
     for d in range(2):
@@ -492,6 +507,7 @@
             sums[i, x] = total[:24]
 
     top_wait(0, ms)
+    top_wait(1, ms)
     sent(temp_x + temp_y + temp_z + state_x + state_y + rate_x + rate_y + edges)
     wait(planes)
 
@@ -529,10 +545,10 @@
         ends[i] = total
         ends[i, pl.ds(COEF, 1), :] = below[COEF : COEF + 1]
 
-    speed[...] = jnp.broadcast_to(jnp.max(top_gather(1), axis=1, keepdims=True), (8, LZ))
+    speed[...] = jnp.broadcast_to(jnp.max(top_gather(2), axis=1, keepdims=True), (8, LZ))
     locals_[6].wait()
 
-    top_wait(1, ms)
+    top_wait(2, ms)
     sent(planes)
 
 
@@ -680,14 +696,14 @@
                 vmem((2, 8, LZ), F32),
                 vmem((2, 8, PW), F32),
                 vmem((2, 8, PW), F32),
-                vmem((2, max(nx * ny, nz), 1, LZ), F32),
+                vmem((3, max(nx * ny, 8), 1, LZ), F32),
                 vmem((EX * EY, 16, LZ), BF16),
                 vmem((96, 128), BF16),
                 pltpu.SemaphoreType.DMA((7,)),
                 pltpu.SemaphoreType.DMA((20,)),
                 pltpu.SemaphoreType.DMA((20,)),
-                pltpu.SemaphoreType.DMA((2,)),
-                pltpu.SemaphoreType.DMA((2,)),
+                pltpu.SemaphoreType.DMA((3,)),
+                pltpu.SemaphoreType.DMA((3,)),
             ],
             compiler_params=pltpu.CompilerParams(
                 collective_id=0, has_side_effects=True, vmem_limit_bytes=24 * 1024 * 1024

time: 35.4 us -> 34.6 us (0.977)
  Pallas kernels: 34.7 us -> 33.8 us
    pallas_call x1, Pallas kernels: 31.8 us -> 31 us  [shards(): pl.pallas_call(functools.partial(exchange, sizes), out_shape=(vmem((8 * N...]
where the time goes in v4:
time: 34.6 us; the launch traced here: 34.5 us
  Pallas kernels  33.8 us (98%)
  between operations  0.64 us (2%)
    pallas_call x1, Pallas kernels, shards(): pl.pallas_call(functools.partial(exchange, sizes), out_shape=(vmem((8 * N...  31 us
    pallas_call x1, Pallas kernels, shards(): pl.pallas_call(finish, out_shape=(pltpu.HBM((NODES, LZ), F32), pltpu.HBM(...  2.83 us

profile of v4, /device:TPU:1, one launch (start us, length us, event | category | flops | bytes accessed | tf_op | source)
XLA Modules:
  0.0 34.5 jit_solution(15807428511089011408)
XLA Ops:
  0.6 31.0 %shard_map.86 = (f32[1024,128]{1,0:T(8,128)S(1)}, s32[128,128]{1,0:T(8,128)S(1)}, f32[153,96,128]{2,1,0:T(8,128)S(1)}, f32[128,8,128]{2,1,0:T(8,128)S(1)}, f32[2...) custom-call(f32[4]{0:T(128)} %rheo_in.1, ...), custom_call_target="tpu_custom_call" | custom-call | tf_op jit(solution)/shard_map/pallas_call | solution.py:665
  31.6 2.8 %shard_map.87 = (f32[128,128]{1,0:T(8,128)}, f32[4,128,128]{2,1,0:T(8,128)}) custom-call(f32[1024,128]{1,0:T(8,128)S(1)} %get-tuple-element.13.nat, s32[128,128]{1,0:T(8,128)S(1)} %get-tuple-element.14.mk, f32[153,96,128]{2,1,0:T(8,128)S(1)} %get-tuple-element.15.f, f32[128,8,128]{2,1,0:T(8,128)S(1)} %get-tuple-element.16.f2, ...), custom_call_target="tpu_custom_call" | custom-call | tf_op jit(solution)/shard_map/pallas_call | solution.py:720

commit v5 on v4

--- a/solution.py
+++ b/solution.py
@@ -188,6 +188,22 @@
     stz[0] = low
     stz[1] = high
 
+    locals_[2].wait()
+    locals_[3].wait()
+    locals_[4].wait()
+
+    for i in range(NODES // 8):
+        label = rk[pl.ds(i * 8, 8), :]
+        total = jnp.zeros((8, LZ), F32)
+        for k in range(4):
+            total = total + jnp.where(label == k, rheo[k], 0.0)
+        nat[pl.ds(COEF * NODES + i * 8, 8), :] = total
+    for d in range(2):
+        xs, ys = (0, LX - 1)[d], (0, LY - 1)[d]
+        for k in range(5):
+            sx[d, pl.ds(k * LY, LY), :] = nat[pl.ds(k * NODES + xs * LY, LY), :]
+            sy[d, pl.ds(k * LX, LX), :] = nat[pl.ds(k * NODES + ys, LX, stride=LY), :]
+
     pl.semaphore_wait(barrier, greeted)
 
     def top_send(i):
@@ -278,25 +294,8 @@
             def _():
                 send().wait_send()
 
+    start(temp_y + temp_x + temp_z)
     top_send(0)
-    start(temp_y + temp_x + temp_z)
-
-    locals_[2].wait()
-    locals_[3].wait()
-    locals_[4].wait()
-
-    for i in range(NODES // 8):
-        label = rk[pl.ds(i * 8, 8), :]
-        total = jnp.zeros((8, LZ), F32)
-        for k in range(4):
-            total = total + jnp.where(label == k, rheo[k], 0.0)
-        nat[pl.ds(COEF * NODES + i * 8, 8), :] = total
-    for d in range(2):
-        xs, ys = (0, LX - 1)[d], (0, LY - 1)[d]
-        for k in range(5):
-            sx[d, pl.ds(k * LY, LY), :] = nat[pl.ds(k * NODES + xs * LY, LY), :]
-            sy[d, pl.ds(k * LX, LX), :] = nat[pl.ds(k * NODES + ys, LX, stride=LY), :]
-
     start(state_y + state_x)
 
     row = lax.broadcasted_iota(jnp.int32, (32, 32), 0)
@@ -643,9 +642,9 @@
         return carry
 
     puts = [put_t]
-    for h in range(2):
-        lax.fori_loop(h * LX // 2, (h + 1) * LX // 2, node_row, 0)
-        part = pl.ds(h * NODES // 2, NODES // 2)
+    for h in range(4):
+        lax.fori_loop(h * LX // 4, (h + 1) * LX // 4, node_row, 0)
+        part = pl.ds(h * NODES // 4, NODES // 4)
         puts.append(pltpu.make_async_copy(res.at[:, part], out_r.at[:, part], osem.at[1 + h]))
         puts[-1].start()
     for put in puts:
@@ -728,7 +727,7 @@
                 vmem((8, PW), F32),
                 vmem((NODES, LZ), F32),
                 vmem((4, NODES, LZ), F32),
-                pltpu.SemaphoreType.DMA((3,)),
+                pltpu.SemaphoreType.DMA((5,)),
             ],
             compiler_params=pltpu.CompilerParams(vmem_limit_bytes=24 * 1024 * 1024),
         )(*(pltpu.with_memory_space_constraint(a, vmem) for a in kept))

time: 34.6 us -> 35.3 us (1.020)
  Pallas kernels: 33.8 us -> 34.5 us
    pallas_call x1, Pallas kernels: 31 us -> 31.7 us  [shards(): pl.pallas_call(functools.partial(exchange, sizes), out_shape=(vmem((8 * N...]
where the time goes in v5:
time: 35.3 us; the launch traced here: 35.2 us
  Pallas kernels  34.5 us (98%)
  between operations  0.64 us (2%)
    pallas_call x1, Pallas kernels, shards(): pl.pallas_call(functools.partial(exchange, sizes), out_shape=(vmem((8 * N...  31.7 us
    pallas_call x1, Pallas kernels, shards(): pl.pallas_call(finish, out_shape=(pltpu.HBM((NODES, LZ), F32), pltpu.HBM(...  2.82 us

profile of v5, /device:TPU:1, one launch (start us, length us, event | category | flops | bytes accessed | tf_op | source)
XLA Modules:
  0.0 35.2 jit_solution(7373006854993423765)
XLA Ops:
  0.6 31.7 %shard_map.86 = (f32[1024,128]{1,0:T(8,128)S(1)}, s32[128,128]{1,0:T(8,128)S(1)}, f32[153,96,128]{2,1,0:T(8,128)S(1)}, f32[128,8,128]{2,1,0:T(8,128)S(1)}, f32[2...) custom-call(f32[4]{0:T(128)} %rheo_in.1, ...), custom_call_target="tpu_custom_call" | custom-call | tf_op jit(solution)/shard_map/pallas_call | solution.py:664
  32.3 2.8 %shard_map.87 = (f32[128,128]{1,0:T(8,128)}, f32[4,128,128]{2,1,0:T(8,128)}) custom-call(f32[1024,128]{1,0:T(8,128)S(1)} %get-tuple-element.13.nat, s32[128,128]{1,0:T(8,128)S(1)} %get-tuple-element.14.mk, f32[153,96,128]{2,1,0:T(8,128)S(1)} %get-tuple-element.15.f, f32[128,8,128]{2,1,0:T(8,128)S(1)} %get-tuple-element.16.f2, ...), custom_call_target="tpu_custom_call" | custom-call | tf_op jit(solution)/shard_map/pallas_call | solution.py:719

commit v6 on v2

--- a/solution.py
+++ b/solution.py
@@ -73,6 +73,18 @@
     has_y = (gy > 0, gy < ny - 1)
     has_z = (gz > 0, gz < nz - 1)
 
+    locals_ = [
+        pltpu.make_async_copy(rate, vel, lsem.at[0]),
+        pltpu.make_async_copy(heat, nat.at[pl.ds(TEMP * NODES, NODES)], lsem.at[1]),
+        pltpu.make_async_copy(guess, nat.at[pl.ds(0, 4 * NODES)], lsem.at[2]),
+        pltpu.make_async_copy(rock, rk, lsem.at[3]),
+        pltpu.make_async_copy(rheo_in, rheo, lsem.at[4]),
+        pltpu.make_async_copy(ops_in, ops, lsem.at[5]),
+        pltpu.make_async_copy(mask, mk, lsem.at[6]),
+    ]
+    for copy in locals_[:2]:
+        copy.start()
+
     barrier = pltpu.get_barrier_semaphore()
 
     stages = (
@@ -99,16 +111,7 @@
 
         lax.fori_loop(1, size, greet_one, 0)
 
-    locals_ = [
-        pltpu.make_async_copy(rate, vel, lsem.at[0]),
-        pltpu.make_async_copy(heat, nat.at[pl.ds(TEMP * NODES, NODES)], lsem.at[1]),
-        pltpu.make_async_copy(guess, nat.at[pl.ds(0, 4 * NODES)], lsem.at[2]),
-        pltpu.make_async_copy(rock, rk, lsem.at[3]),
-        pltpu.make_async_copy(rheo_in, rheo, lsem.at[4]),
-        pltpu.make_async_copy(ops_in, ops, lsem.at[5]),
-        pltpu.make_async_copy(mask, mk, lsem.at[6]),
-    ]
-    for copy in locals_:
+    for copy in locals_[2:]:
         copy.start()
 
     for d in range(2):

time: 34.1 us -> 34.1 us (level)
  no operation moved by 1% of the time
where the time goes in v6:
time: 34.1 us; the launch traced here: 33.9 us
  Pallas kernels  33.3 us (98%)
  between operations  0.64 us (2%)
    pallas_call x1, Pallas kernels, shards(): pl.pallas_call(functools.partial(exchange, sizes), out_shape=(vmem((8 * N...  30.5 us
    pallas_call x1, Pallas kernels, shards(): pl.pallas_call(finish, out_shape=(pltpu.HBM((NODES, LZ), F32), pltpu.HBM(...  2.83 us

profile of v6, /device:TPU:1, one launch (start us, length us, event | category | flops | bytes accessed | tf_op | source)
XLA Modules:
  0.0 33.9 jit_solution(9981934188514223922)
XLA Ops:
  0.6 30.5 %shard_map.86 = (f32[1024,128]{1,0:T(8,128)S(1)}, s32[128,128]{1,0:T(8,128)S(1)}, f32[153,96,128]{2,1,0:T(8,128)S(1)}, f32[128,8,128]{2,1,0:T(8,128)S(1)}, f32[2...) custom-call(f32[4]{0:T(128)} %rheo_in.1, ...), custom_call_target="tpu_custom_call" | custom-call | tf_op jit(solution)/shard_map/pallas_call | solution.py:632
  31.1 2.8 %shard_map.87 = (f32[128,128]{1,0:T(8,128)}, f32[4,128,128]{2,1,0:T(8,128)}) custom-call(f32[1024,128]{1,0:T(8,128)S(1)} %get-tuple-element.13.nat, s32[128,128]{1,0:T(8,128)S(1)} %get-tuple-element.14.mk, f32[153,96,128]{2,1,0:T(8,128)S(1)} %get-tuple-element.15.f, f32[128,8,128]{2,1,0:T(8,128)S(1)} %get-tuple-element.16.f2, ...), custom_call_target="tpu_custom_call" | custom-call | tf_op jit(solution)/shard_map/pallas_call | solution.py:685
